TPU v7x, 128 devices: a whole 4x4x4 slice. The times are simulated.
128 devices in a mesh: replica: 8 (over x_lo, z), fsdp: 16 (over x_hi, y, core).
Axes of the slice: x: 4 (x_hi: 2, x_lo: 2; x = x_hi * 2 + x_lo), y: 4, z: 4, core: 2. Of those that a mesh axis runs over, the one named last changes fastest.
Arguments:
- local_params: float32 [8, 2048, 4096], P('replica', 'fsdp')
- params: float32 [2048, 4096], P('fsdp')
- momentum: float32 [2048, 4096], P('fsdp'), may hold values from -0.12 to 0.12
- old_mask: int32 [8], replicated, may hold values from 0 to 1, as said below
- attn: bfloat16 [8, 8192, 2048], P('replica', 'fsdp'), may hold values from -6 to 6
- resid: bfloat16 [8, 8192, 4096], P('replica', 'fsdp'), may hold values from -6 to 6
- gain: bfloat16 [4096], replicated, may hold values from 0.5 to 1.5
- out_grad: bfloat16 [8, 8192, 4096], P('replica', 'fsdp'), may hold values from -6 to 6
Outputs:
- new_params: float32 [2048, 4096], P('fsdp', 'replica')
- new_momentum: float32 [2048, 4096], P('fsdp', 'replica')
- weight_grad: bfloat16 [8, 2048, 4096], P('replica', 'fsdp')
- attn_grad: bfloat16 [8, 8192, 2048], P('replica', 'fsdp')
- resid_grad: bfloat16 [8, 8192, 4096], P('replica', 'fsdp')
Inputs may be any that keep to these rules, and one draw needn't show every extreme that they name: `old_mask`: between 1 and 4 entries are 0, at drawn positions.
All inputs are finite; a program needn't handle non-finite values.
Results may differ from a plain program's by a relative error of at most 0.019.
Values may be sent and summed in bfloat16 or wider, within the bound.
A program may use at most 192 MiB of HBM per device.

v0:
```python
import math

import jax
import jax.numpy as jnp
from jax import lax
from jax.sharding import PartitionSpec as P

D = 4096
HQ = 2048


outer_rate = 0.7
outer_beta = 0.9
clip_scale = 0.1


def shards(local_params, params, momentum, old_mask, attn, resid, gain, out_grad):
    rank = lax.axis_index("replica")
    replicas = lax.axis_size("replica")
    shard_rows, width = params.shape
    cols = width // replicas
    limit = clip_scale * math.sqrt(HQ * D)
    delta = params - local_params[0]
    squares = lax.psum(jnp.sum(delta * delta), "fsdp")
    factor = jnp.minimum(jnp.float32(1.0), limit / (jnp.sqrt(squares) + 1e-06))
    is_old = lax.dynamic_index_in_dim(old_mask, rank, 0, keepdims=False).astype(jnp.float32)
    old_count = jnp.sum(old_mask.astype(jnp.float32))
    term = delta * (is_old * factor)
    pseudo = lax.psum(term.astype(jnp.bfloat16), "replica").astype(jnp.float32) / old_count
    full_momentum = outer_beta * momentum + pseudo
    full_params = params - outer_rate * (pseudo + outer_beta * full_momentum)
    mom_out = lax.dynamic_slice_in_dim(full_momentum, rank * cols, cols, 1)
    par_out = lax.dynamic_slice_in_dim(full_params, rank * cols, cols, 1)
    weights = lax.all_gather(full_params.astype(jnp.bfloat16), "fsdp", axis=0, tiled=True)
    attn_rows = attn[0]
    hsum = resid[0].astype(jnp.float32) + jnp.dot(
        attn_rows, weights, preferred_element_type=jnp.float32
    )
    inverse = lax.rsqrt(jnp.mean(hsum * hsum, axis=-1, keepdims=True) + 1e-05)
    scaled = out_grad[0].astype(jnp.float32) * gain.astype(jnp.float32)
    project = jnp.mean(scaled * hsum, axis=-1, keepdims=True)
    hgrad = (inverse * scaled - hsum * inverse**3 * project).astype(jnp.bfloat16)
    agrad = lax.dot_general(
        hgrad, weights, (((1,), (1,)), ((), ())), preferred_element_type=jnp.float32
    ).astype(jnp.bfloat16)
    wgrad = lax.psum_scatter(
        lax.dot_general(
            attn_rows, hgrad, (((0,), (0,)), ((), ())), preferred_element_type=jnp.float32
        ).astype(jnp.bfloat16),
        "fsdp",
        scatter_dimension=0,
        tiled=True,
    )
    return (par_out, mom_out, wgrad[None], agrad[None], hgrad[None])


def solution(mesh):
    return jax.shard_map(
        shards,
        mesh=mesh,
        in_specs=(
            P("replica", "fsdp", None),
            P("fsdp", None),
            P("fsdp", None),
            P(),
            P("replica", "fsdp", None),
            P("replica", "fsdp", None),
            P(),
            P("replica", "fsdp", None),
        ),
        out_specs=(
            P("fsdp", "replica"),
            P("fsdp", "replica"),
            P("replica", "fsdp", None),
            P("replica", "fsdp", None),
            P("replica", "fsdp", None),
        ),
        check_vma=False,
    )
```

profile of v0, /device:TPU:1, one launch (start us, length us, event | category | flops | bytes accessed | tf_op | source)
XLA Modules:
  0.0 456.8 jit_solution(16276554256119920867)
XLA Ops:
  7.2 0.0 all-reduce.2.cloned.1.call-start
  7.2 1.4 dynamic_slice.10
  8.6 3.4 multiply_reduce_fusion.1
  12.6 34.9 %psum.14 = f32[]{:T(128)} all-reduce(f32[]{:T(128)} %multiply_reduce_fusion.1), channel_id=1, replica_groups=mesh['replica'=8,'fsdp'=16] {'fsdp'}, use_global_device_ids=true, to_apply=%region_1.0 | all-reduce | flops 1 | bytes 8 | tf_op jit(solution)/shard_map/psum | solution.py:24
  48.3 3.4 multiply_convert_fusion
  51.7 0.0 all-gather.2.cloned.1.call-start
  51.8 0.6 convert_reduce_fusion
  52.4 74.2 %all-reduce.2.cloned.1.call-done = bf16[128,4096]{1,0:T(8,128)(2,1)} async-done(((bf16[128,4096]{1,0:T(8,128)(2,1)}), bf16[128,4096]{1,0:T(8,128)(2,1)}) %all-reduce.2.cloned.1.call-update) | async-done | bytes 1048592 | tf_op jit(solution)/shard_map/psum | solution.py:29
  126.6 6.3 %fusion.8 = (bf16[128,4096]{1,0:T(8,128)(2,1)}, f32[128,4096]{1,0:T(8,128)}, f32[128,4096]{1,0:T(8,128)}) fusion(f32[128,4096]{1,0:T(8,128)} %param.9, f32[128,4096]{1,0:T(8,128)} %param.10, f32[]{:T(128)} %convert_reduce_fusion, bf16[128,4096]{1,0:T(8,128)(2,1)} %all-reduce.2.cloned.1.call-done), kind=kLoop, calls=%fused_computation.25 | loop fusion | flops 4718592 | bytes 10485764 | tf_op jit(solution)/shard_map/convert_element_type | solution.py:34
  132.9 0.0 reduce-scatter.4.cloned.1.call-start
  133.0 6.4 %copy.18 = bf16[1,512,4096]{1,2,0:T(8,128)(2,1)} copy(bf16[1,512,4096]{2,1,0:T(8,128)(2,1)} %param.15) | data formatting | bytes 8388608 | tf_op args[7]
  139.4 6.5 %copy.17 = bf16[1,512,4096]{1,2,0:T(8,128)(2,1)} copy(bf16[1,512,4096]{2,1,0:T(8,128)(2,1)} %param.13) | data formatting | bytes 8388608 | tf_op args[5]
  145.9 101.3 %all-gather.2.cloned.1.call-done = bf16[2048,4096]{1,0:T(8,128)(2,1)} async-done(((bf16[128,4096]{1,0:T(8,128)(2,1)}), bf16[2048,4096]{1,0:T(8,128)(2,1)}) %all-gather.2.cloned.1.call-update) | async-done | bytes 16777232 | tf_op jit(solution)/shard_map/all_gather | solution.py:34
  247.2 17.6 %multiply_reduce_fusion = (f32[512]{0:T(512)S(1)}, f32[512]{0:T(512)S(1)}, f32[512,4096]{0,1:T(8,128)}) fusion(f32[4096]{0:T(1024)S(1)} %convert_element_type.55, bf16[1,512,4096]{1,2,0:T(8,128)(2,1)} %copy.18, bf16[2048,4096]{1,0:T(8,128)(2,1)} %all-gather.2.cloned.1.call-done, bf16[1,512,2048]{2,1,0:T(8,128)(2,1)S(1)} %copy-done, ...), kind=kOutput, calls=%fused_computation.8 | convolution fusion | flops 8606711808 | bytes 35672064 | tf_op jit(solution)/shard_map/dot_general | solution.py:36
  264.8 4.5 fusion.3
  269.2 2.0 copy-done.2
  271.3 11.6 %convert_bitcast_fusion = bf16[2048,4096]{0,1:T(8,128)(2,1)} fusion(bf16[512,4096]{0,1:T(8,128)(2,1)S(1)} %fusion.3, bf16[1,512,2048]{2,1,0:T(8,128)(2,1)S(1)} %copy-done), kind=kOutput, calls=%fused_computation | convolution fusion | flops 8598323200 | bytes 23068672 | tf_op jit(solution)/shard_map/dot_general | solution.py:47
  282.9 20.7 %copy.21 = bf16[2048,4096]{1,0:T(8,128)(2,1)} copy(bf16[2048,4096]{0,1:T(8,128)(2,1)} %convert_bitcast_fusion) | data formatting | bytes 33554432
  303.6 1.9 constant_dynamic-slice_fusion
  305.5 6.4 %copy.20 = bf16[1,512,4096]{2,1,0:T(8,128)(2,1)} copy(bf16[1,512,4096]{1,2,0:T(8,128)(2,1)} %bitcast.34) | data formatting | bytes 8388608
  311.9 17.1 %fusion.5 = bf16[1,512,2048]{2,1,0:T(8,128)(2,1)} fusion(bf16[512,4096]{0,1:T(8,128)(2,1)} %copy-done.2, bf16[2048,4096]{1,0:T(8,128)(2,1)} %all-gather.2.cloned.1.call-done), kind=kOutput, calls=%fused_computation.10 | convolution fusion | flops 8590983168 | bytes 23068672 | tf_op jit(solution)/shard_map/dot_general | solution.py:43
  329.0 118.3 %reduce-scatter.4.cloned.1.call-done = bf16[128,4096]{1,0:T(8,128)(2,1)} async-done(((bf16[2048,4096]{1,0:T(8,128)(2,1)}), bf16[128,4096]{1,0:T(8,128)(2,1)}) %reduce-scatter.4.cloned.1.call-update) | async-done | bytes 1048592
  447.4 1.6 copy.22
  449.0 1.3 copy.19
  (16 shorter events, 0.1 us)
Async XLA Ops:
  7.2 240.0 %copy-start = (bf16[1,512,2048]{2,1,0:T(8,128)(2,1)S(1)}, bf16[1,512,2048]{2,1,0:T(8,128)(2,1)}, u32[]{:S(2)}) copy-start(bf16[1,512,2048]{2,1,0:T(8,128)(2,1)} %param.12) | copy-start | bytes 6291460
  7.2 119.4 %all-reduce.2.cloned.1.call-start = ((), (), s32[]{:S(2)}) async-start(), calls=%async_computation.1 | async-start | bytes 2097152 | tf_op jit(solution)/shard_map/psum | solution.py:29
  12.0 39.8 %copy-start.5 = (s32[8]{0:T(128)S(1)}, s32[8]{0:T(128)}, u32[]{:S(2)}) copy-start(s32[8]{0:T(128)} %param.11) | copy-start | bytes 100
  51.7 195.4 %all-gather.2.cloned.1.call-start = ((), (), s32[]{:S(2)}) async-start(), calls=%async_computation.2 | async-start | bytes 17825792 | tf_op jit(solution)/shard_map/all_gather | solution.py:34
  52.4 80.6 %copy-start.4 = (bf16[4096]{0:T(1024)(128)(2,1)S(1)}, bf16[4096]{0:T(1024)(128)(2,1)}, u32[]{:S(2)}) copy-start(bf16[4096]{0:T(1024)(128)(2,1)} %param.14) | copy-start | bytes 24580
  132.9 314.5 %reduce-scatter.4.cloned.1.call-start = ((), (), s32[]{:S(2)}) async-start(), calls=%async_computation.3 | async-start | bytes 17825792
  247.1 17.6 %copy-start.3 = (bf16[1,512,4096]{1,2,0:T(8,128)(2,1)S(1)}, bf16[1,512,4096]{1,2,0:T(8,128)(2,1)}, u32[]{:S(2)}) copy-start(bf16[1,512,4096]{1,2,0:T(8,128)(2,1)} %copy.18) | copy-start | bytes 12582916
  269.2 2.0 copy-start.2
  311.9 138.4 %copy-start.1 = (bf16[1,512,2048]{2,1,0:T(8,128)(2,1)S(1)}, bf16[1,512,2048]{2,1,0:T(8,128)(2,1)}, u32[]{:S(2)}) copy-start(bf16[1,512,2048]{2,1,0:T(8,128)(2,1)} %param.12) | copy-start | bytes 6291460
Sparse Core Ops, SparseCore 0:
  51.8 74.6 all-reduce.1
  133.0 114.0 all-gather.1
  303.7 143.5 reduce-scatter.3
where the time goes:
time: 458 us; the launch traced here: 457 us
  waiting for transfers between devices  294 us (64%)
  local copies, waits for them, and re-layouts  48.2 us (11%)
  matrix products  46.4 us (10%)
  blocking collectives  34.9 us (8%)
  other arithmetic  18.2 us (4%)
  between operations  15.2 us (3%)
    unnamed x4, waiting for transfers between devices  118 us
    all_gather x1, waiting for transfers between devices, shards(): lax.all_gather(full_params.astype(jnp.bfloat16), 'fsdp', axis=0, tiled=True)  101 us
    psum x1, waiting for transfers between devices, shards(): lax.psum(term.astype(jnp.bfloat16), 'replica').astype(jnp.float32)  74.2 us
    unnamed x18, local copies, waits for them, and re-layouts  45 us
    psum x1, blocking collectives, shards(): squares = lax.psum(jnp.sum(delta * delta), 'fsdp')  34.9 us
    dot_general x1, matrix products, shards(): jnp.dot(attn_rows, weights, preferred_element_type=jnp.float32)  17.6 us
    dot_general x1, matrix products, shards(): lax.dot_general(hgrad, weights, (((1,), (1,)), ((), ())), preferred_eleme...  17.1 us
    dot_general x1, matrix products, shards(): lax.dot_general(attn_rows, hgrad, (((0,), (0,)), ((), ())), preferred_ele...  11.6 us
  transfers between devices with their start and end apart: 3, of which 3 were waited for; matrix products, arithmetic and copies ran while one was open for 9% of the time, Pallas kernels for 0%

commit v1 on v0

v1 whole, which is shorter than its diff:
```python
import functools
import math

import jax
import jax.numpy as jnp
from jax import lax
from jax.experimental import pallas as pl
from jax.experimental.pallas import tpu as pltpu
from jax.sharding import PartitionSpec as P

D = 4096
HQ = 2048
TOK = 512

outer_rate = 0.7
outer_beta = 0.9
clip_scale = 0.1
BF16_MAX = float(jnp.finfo(jnp.bfloat16).max)

MESH = pl.DeviceIdType.MESH
BF = jnp.bfloat16
F32 = jnp.float32

PARTS = (
    (0, 96, 48, ("x", "y", "z")),
    (96, 80, 48, ("y", "z", "x")),
    (176, 80, 32, ("z", "x", "y")),
)
Y_UNITS = 5
X_UNITS = 3


def place():
    r = lax.axis_index("replica")
    f = lax.axis_index("fsdp")
    x = (f // 8) * 2 + r // 4
    return x, lax.rem(f // 2, 4), lax.rem(r, 4), lax.rem(f, 2)


def device(x, y, z, c):
    return (lax.rem(x, 2) * 4 + z, (x // 2) * 8 + y * 2 + c)


def up(i, n=4):
    return lax.rem(i + 1, n)


def down(i, n=4):
    return lax.rem(i + n - 1, n)


def remote(src, dst, send, recv, target):
    return pltpu.make_async_remote_copy(
        src_ref=src, dst_ref=dst, send_sem=send, recv_sem=recv, device_id=target, device_id_type=MESH
    )


def greet(targets):
    barrier = pltpu.get_barrier_semaphore()
    for target in targets:
        pl.semaphore_signal(barrier, inc=1, device_id=target, device_id_type=MESH)
    pl.semaphore_wait(barrier, len(targets))


def outer_kernel(
    lp, params, momentum, mask, attn, resid, gain, og,
    par_out, mom_out, w_out, hg_out, at_out,
    lv, pv, mv, dsend, drecv, nsend, nrecv, fsend, frecv, wb, w5, av, rv, ov, hs, hg, atv, stats, st_own, st_other,
    load_sem, mom_sem, d_send, d_recv, n_send, n_recv, f_send, f_recv, w_send, w_recv,
    act_own, act_send, act_recv, g_send, g_recv, s_send, s_recv, out_sem,
):
    x, y, z, c = place()
    r = lax.axis_index("replica")
    f = lax.axis_index("fsdp")
    other = 1 - c
    sibling = device(x, y, z, other)

    order = (4, 1, 2, 3, 5, 6, 7, 0)
    for k in order:
        cols = pl.ds(pl.multiple_of(lax.rem(r + k, 8) * 512, 512), 512)
        pltpu.make_async_copy(lp.at[:, cols], lv.at[k], load_sem.at[0, k]).start()
        pltpu.make_async_copy(params.at[:, cols], pv.at[k], load_sem.at[1, k]).start()
    own_cols = pl.ds(pl.multiple_of(r * 512, 512), 512)
    mom_copy = pltpu.make_async_copy(momentum.at[:, own_cols], mv, mom_sem)
    mom_copy.start()

    targets = [(lax.rem(r + k, 8), f) for k in range(1, 8)]
    targets += [(r, lax.rem(f + j, 16)) for j in range(1, 16)]
    outside = jnp.where(lax.rem(x, 2) == 0, down(x), up(x))
    targets.append(device(outside, y, z, c))
    greet(targets)

    squares = jnp.zeros((8, 512), F32)
    delta_copies = []
    for k in order:
        pltpu.make_async_copy(lv.at[k], lv.at[k], load_sem.at[0, k]).wait()
        pltpu.make_async_copy(pv.at[k], pv.at[k], load_sem.at[1, k]).wait()
        delta = pv[k] - lv[k]
        squares = squares + jnp.sum((delta * delta).reshape(16, 8, 512), axis=0)
        block = jnp.clip(delta, -BF16_MAX, BF16_MAX).astype(BF)
        if k == 0:
            drecv[0] = block
        else:
            dsend[k] = block
            copy = remote(
                dsend.at[k], drecv.at[k], d_send.at[k], d_recv.at[k], (lax.rem(r + k, 8), f)
            )
            copy.start()
            delta_copies.append(copy)

    tile = squares[:, 0:128] + squares[:, 128:256] + squares[:, 256:384] + squares[:, 384:512]
    nsend[...] = tile
    nrecv[0] = tile
    norm_copies = []
    for j in range(1, 16):
        copy = remote(nsend, nrecv.at[j], n_send.at[j], n_recv.at[j], (r, lax.rem(f + j, 16)))
        copy.start()
        norm_copies.append(copy)

    mine = pl.ds(pl.multiple_of(c * TOK, TOK), TOK)
    act_copies = []
    attn_own = pltpu.make_async_copy(attn, av.at[mine], act_own.at[0])
    attn_send = remote(attn, av.at[mine], act_send.at[0], act_recv.at[0], sibling)
    attn_own.start()
    attn_send.start()
    for k in range(8):
        for s, (src, dst) in enumerate(((resid, rv), (og, ov))):
            here = pl.ds(pl.multiple_of(k * 512 + c * 256, 256), 256)
            there = pl.ds(pl.multiple_of(k * 512 + other * 256, 256), 256)
            i = 1 + 2 * k + s
            a = pltpu.make_async_copy(src.at[:, here], dst.at[k, mine], act_own.at[i])
            b = remote(src.at[:, there], dst.at[k, mine], act_send.at[i], act_recv.at[i], sibling)
            a.start()
            b.start()
            act_copies.append((a, b))

    for copy in norm_copies:
        copy.wait_recv()
    total = jnp.full((8, 128), jnp.sum(nrecv[...]), F32)
    fsend[...] = total
    frecv[0] = total
    factor_copies = []
    for k in range(1, 8):
        copy = remote(fsend, frecv.at[k], f_send.at[k], f_recv.at[k], (lax.rem(r + k, 8), f))
        copy.start()
        factor_copies.append(copy)
    for copy in factor_copies:
        copy.wait_recv()
    limit = clip_scale * math.sqrt(HQ * D)
    factors = jnp.minimum(F32(1.0), limit / (jnp.sqrt(frecv[...]) + 1e-06))
    count = F32(0.0)
    for k in range(8):
        count = count + mask[k].astype(F32)

    pseudo = jnp.zeros((128, 512), F32)
    for copy in delta_copies:
        copy.wait_recv()
    for k in range(8):
        weight = mask[lax.rem(r + 8 - k, 8)].astype(F32) * jnp.max(factors[k])
        pseudo = pseudo + drecv[k].astype(F32) * weight
    pseudo = pseudo / count
    mom_copy.wait()
    new_mom = outer_beta * mv[...] + pseudo
    new_par = pv[0] - outer_rate * (pseudo + outer_beta * new_mom)
    mom_out[...] = new_mom
    par_out[...] = new_par
    rounded = new_par.astype(BF)
    wb[0] = rounded[:, 0:256]
    wb[1] = rounded[:, 256:512]

    rows = pl.ds(pl.multiple_of(c * 128, 128), 128)
    swap = remote(wb.at[other], w5.at[x, z, y, rows], w_send, w_recv, sibling)
    swap.start()
    w5[x, z, y, rows, :] = wb[c]
    swap.wait_recv()

    index = {"x": x, "y": y, "z": z}

    def region(part, gathered, axis, i, half):
        start, size, cut, _ = PARTS[part]
        if half == 0:
            size = cut
        elif half == 1:
            start, size = start + cut, size - cut
        at = {a: (slice(None) if a in gathered else index[a]) for a in "xyz"}
        at[axis] = i
        return w5.at[at["x"], at["z"], at["y"], pl.ds(start, size), :]

    gather_copies = []

    def send(phase, part, kind, ref, axis, i):
        place_there = dict(index)
        place_there[axis] = i
        sem = (phase * 3 + part) * 4 + kind
        copy = remote(
            ref, ref, g_send.at[sem], g_recv.at[sem],
            device(place_there["x"], place_there["y"], place_there["z"], c),
        )
        copy.start()
        gather_copies.append(copy)

    def arrived(phase, part, kind, ref):
        sem = (phase * 3 + part) * 4 + kind
        pltpu.make_async_copy(ref, ref, g_recv.at[sem]).wait()

    for phase in range(3):
        for part in range(3):
            axes = PARTS[part][3]
            axis, gathered = axes[phase], axes[:phase]
            i = index[axis]
            own = region(part, gathered, axis, i, None)
            send(phase, part, 0, own, axis, up(i))
            send(phase, part, 1, own, axis, down(i))
        if phase == 2:
            attn_own.wait()
            attn_send.wait_recv()

            @pl.loop(0, 32)
            def _(t):
                tok = pl.ds(pl.multiple_of(lax.rem(t, 4) * 256, 256), 256)
                col = pl.ds(pl.multiple_of((t // 4) * 256, 256), 256)
                atv[t // 4, :, tok] = av[tok, col].T

            at_copy = pltpu.make_async_copy(atv, at_out, out_sem.at[0])
            at_copy.start()
        for part in range(3):
            axes = PARTS[part][3]
            axis, gathered = axes[phase], axes[:phase]
            i = index[axis]
            left = region(part, gathered, axis, down(i), None)
            right = region(part, gathered, axis, up(i), None)
            arrived(phase, part, 0, left)
            send(phase, part, 2, region(part, gathered, axis, down(i), 0), axis, up(i))
            arrived(phase, part, 1, right)
            send(phase, part, 3, region(part, gathered, axis, up(i), 1), axis, down(i))
        for part in range(3):
            axes = PARTS[part][3]
            axis, gathered = axes[phase], axes[:phase]
            far = lax.rem(index[axis] + 2, 4)
            arrived(phase, part, 2, region(part, gathered, axis, far, 0))
            arrived(phase, part, 3, region(part, gathered, axis, far, 1))

    w_copy = pltpu.make_async_copy(w5, w_out, out_sem.at[1])
    w_copy.start()

    for a, b in act_copies:
        a.wait()
        b.wait_recv()
    stats[...] = jnp.zeros_like(stats)

    @pl.loop(0, 16)
    def _(t):
        k = t // 2
        tok = pl.ds(pl.multiple_of(lax.rem(t, 2) * 512, 512), 512)
        top = w5[k // 4, lax.rem(k, 4)].reshape(1024, 256)
        bottom = w5[k // 4 + 2, lax.rem(k, 4)].reshape(1024, 256)
        h = jnp.dot(av[tok, 0:1024], top, preferred_element_type=F32)
        h = h + jnp.dot(av[tok, 1024:2048], bottom, preferred_element_type=F32)
        h = h + rv[k, tok, :].astype(F32)
        hs[k, tok, :] = h
        sc = ov[k, tok, :].astype(F32) * gain[2 * k + c]
        hh = h * h
        sh = sc * h
        stats[0, tok, :] += hh[:, 0:128] + hh[:, 128:256]
        stats[1, tok, :] += sh[:, 0:128] + sh[:, 128:256]

    lane = lax.broadcasted_iota(jnp.int32, (256, 128), 1)

    @pl.loop(0, 4)
    def _(t):
        tok = pl.ds(pl.multiple_of(t * 256, 256), 256)
        a = jnp.sum(stats[0, tok, :], axis=1, keepdims=True)
        b = jnp.sum(stats[1, tok, :], axis=1, keepdims=True)
        st_own[tok, :] = jnp.where(lane < 64, a, b)

    st_copy = remote(st_own, st_other, s_send, s_recv, sibling)
    st_copy.start()
    st_copy.wait_recv()

    @pl.loop(0, 4)
    def _(t):
        tok = pl.ds(pl.multiple_of(t * 256, 256), 256)
        both = (st_own[tok, :] + st_other[tok, :]) * (1.0 / D)
        inv = lax.rsqrt(both[:, 0:1] + 1e-05)
        slope = inv * inv * inv * both[:, 64:65]
        for k in range(8):
            sc = ov[k, tok, :].astype(F32) * gain[2 * k + c]
            hg[k, tok, :] = (inv * sc - hs[k, tok, :] * slope).astype(BF)

    hg_copy = pltpu.make_async_copy(hg, hg_out, out_sem.at[2])
    hg_copy.start()

    for copy in delta_copies + norm_copies + factor_copies + gather_copies + [swap, st_copy, attn_send]:
        copy.wait_send()
    for _, b in act_copies:
        b.wait_send()
    at_copy.wait()
    w_copy.wait()
    hg_copy.wait()


def grad_kernel(
    at, hgr, w,
    wg_out, ag_out, hg_out,
    atv, hgv, w5, part, ry, ryx, rx, rxy, fin, agf, ags, agr,
    load_sem, y_send, y_recv, yx_send, yx_recv, x_send, x_recv, xy_send, xy_recv,
    fin_send, fin_recv, ag_send, ag_recv, hgo_own, hgo_send, hgo_recv,
):
    x, y, z, c = place()
    other = 1 - c
    xh = x // 2
    xo = 1 - xh
    sibling = device(x, y, z, other)
    yr, yl, yo = up(y), down(y), lax.rem(y + 2, 4)
    right, left = device(x, yr, z, c), device(x, yl, z, c)
    across = device(lax.rem(x + 2, 4), y, z, c)

    at_load = pltpu.make_async_copy(at, atv, load_sem.at[0])
    hg_load = pltpu.make_async_copy(hgr, hgv, load_sem.at[1])
    w_load = pltpu.make_async_copy(w, w5, load_sem.at[2])
    at_load.start()
    hg_load.start()
    w_load.start()
    greet([sibling, right, left, across])
    at_load.wait()
    hg_load.wait()

    def comp(k, h, d):
        acc = jnp.dot(atv[h * 4 + d], hgv[k], preferred_element_type=F32)
        part[k, h, d] = acc.astype(BF).reshape(2, 128, 256)

    def y_copy(u, m):
        d, h = ((yo, 0), (yo, 1), (yr, 1), (yl, 0), (yr, 0), (yl, 1))[m]
        target = right if m % 2 == 0 else left
        return remote(part.at[u, :, d, h], ry.at[u, m], y_send.at[u, m], y_recv.at[u, m], target)

    def yx_copy(u):
        return remote(part.at[u, xo, y], ryx.at[u], yx_send.at[u], yx_recv.at[u], across)

    def x_copy(v):
        return remote(part.at[Y_UNITS + v, xo], rx.at[v], x_send.at[v], x_recv.at[v], across)

    def xy_copy(v, m):
        d, h = ((yo, 0), (yo, 1), (yr, 1), (yl, 0), (yr, 0), (yl, 1))[m]
        target = right if m % 2 == 0 else left
        return remote(
            part.at[Y_UNITS + v, xh, d, h], rxy.at[v, m], xy_send.at[v, m], xy_recv.at[v, m], target
        )

    def x_start(v):
        for d in range(4):
            comp(Y_UNITS + v, xo, d)
        x_copy(v).start()

    def y_start(u):
        comp(u, 0, yo)
        comp(u, 1, yo)
        y_copy(u, 0).start()
        y_copy(u, 1).start()

    @pl.loop(0, X_UNITS)
    def _(v):
        x_start(v)
        y_start(v)

    @pl.loop(X_UNITS, Y_UNITS)
    def _(u):
        y_start(u)

    @pl.loop(0, Y_UNITS)
    def _(u):
        comp(u, 0, yr)
        comp(u, 1, yr)
        y_copy(u, 2).start()
        comp(u, 0, yl)
        comp(u, 1, yl)
        y_copy(u, 3).start()

    mine = pl.ds(pl.multiple_of(c * TOK, TOK), TOK)
    theirs = pl.ds(pl.multiple_of(other * TOK, TOK), TOK)

    def hgo_copies(k):
        cols = pl.ds(pl.multiple_of(k * 512 + c * 256, 256), 256)
        return (
            pltpu.make_async_copy(hgv.at[k, mine], hg_out.at[:, cols], hgo_own.at[k]),
            remote(hgv.at[k, theirs], hg_out.at[:, cols], hgo_send.at[k], hgo_recv.at[k], sibling),
        )

    @pl.loop(0, 8)
    def _(k):
        a, b = hgo_copies(k)
        a.start()
        b.start()

    @pl.loop(0, Y_UNITS)
    def _(u):
        comp(u, 0, y)
        comp(u, 1, y)

    @pl.loop(0, X_UNITS)
    def _(v):
        for d in range(4):
            comp(Y_UNITS + v, xh, d)

    def add(dst, src):
        part[dst] = (part[dst].astype(F32) + src.astype(F32)).astype(BF)

    @pl.loop(0, Y_UNITS)
    def _(u):
        y_copy(u, 0).wait_recv()
        for h in range(2):
            add((u, h, yr, 0), ry[u, 0, h])
        y_copy(u, 4).start()
        y_copy(u, 1).wait_recv()
        for h in range(2):
            add((u, h, yl, 1), ry[u, 1, h])
        y_copy(u, 5).start()

    def x_middle(v):
        x_copy(v).wait_recv()
        for d in (yo, yr, yl, y):
            for h in range(2):
                add((Y_UNITS + v, xh, d, h), rx[v, d, h])
            if d is yo:
                xy_copy(v, 0).start()
                xy_copy(v, 1).start()
        xy_copy(v, 2).start()
        xy_copy(v, 3).start()

    def y_finish(u):
        for m in (2, 3, 4, 5):
            y_copy(u, m).wait_recv()
        for h in range(2):
            for s, (m, n) in enumerate(((3, 4), (2, 5))):
                total = part[u, h, y, s].astype(F32) + ry[u, m, h].astype(F32) + ry[u, n, h].astype(F32)
                part[u, h, y, s] = total.astype(BF)
        yx_copy(u).start()

    x_middle(0)

    w_load.wait()

    def agrad(q, tok):
        wide = jnp.concatenate([w5[(q // 4) * 2 + k // 4, k % 4, lax.rem(q, 4)] for k in range(8)], axis=1)
        rows = jnp.concatenate([hgv[k, tok, :] for k in range(8)], axis=1)
        return lax.dot_general(rows, wide, (((1,), (1,)), ((), ())), preferred_element_type=F32)

    @pl.loop(0, 8)
    def _(q):
        ags[:, pl.ds(pl.multiple_of(q * 256, 256), 256)] = agrad(q, theirs).astype(BF)

    ag_copy = remote(ags, agr, ag_send, ag_recv, sibling)
    ag_copy.start()

    @pl.loop(0, 8)
    def _(q):
        agf[:, pl.ds(pl.multiple_of(q * 256, 256), 256)] = agrad(q, mine)

    ag_copy.wait_recv()

    @pl.loop(0, 8)
    def _(q):
        col = pl.ds(pl.multiple_of(q * 256, 256), 256)
        ag_out[:, col] = (agf[:, col] + agr[:, col].astype(F32)).astype(BF)

    x_middle(1)
    y_finish(0)
    x_middle(2)

    @pl.loop(1, Y_UNITS)
    def _(u):
        y_finish(u)

    @pl.loop(0, X_UNITS)
    def _(v):
        xy_copy(v, 0).wait_recv()
        add((Y_UNITS + v, xh, yr, 0), rxy[v, 0])
        xy_copy(v, 4).start()
        xy_copy(v, 1).wait_recv()
        add((Y_UNITS + v, xh, yl, 1), rxy[v, 1])
        xy_copy(v, 5).start()

    def fin_copy(k):
        cols = pl.ds(pl.multiple_of(k * 512 + c * 256, 256), 256)
        return remote(fin.at[k, other], wg_out.at[:, cols], fin_send.at[k], fin_recv.at[k], sibling)

    def deliver(k):
        fin_copy(k).start()
        cols = pl.ds(pl.multiple_of(k * 512 + c * 256, 256), 256)
        wg_out[:, cols] = fin[k, c]

    @pl.loop(0, Y_UNITS)
    def _(u):
        yx_copy(u).wait_recv()
        fin[u] = (part[u, xh, y].astype(F32) + ryx[u].astype(F32)).astype(BF)
        deliver(u)

    @pl.loop(0, X_UNITS)
    def _(v):
        for m in (2, 3, 4, 5):
            xy_copy(v, m).wait_recv()
        for s, (m, n) in enumerate(((3, 4), (2, 5))):
            total = part[Y_UNITS + v, xh, y, s].astype(F32) + rxy[v, m].astype(F32) + rxy[v, n].astype(F32)
            fin[Y_UNITS + v, s] = total.astype(BF)
        deliver(Y_UNITS + v)

    @pl.loop(0, 8)
    def _(k):
        copy = fin_copy(k)
        copy.wait_recv()
        copy.wait_send()
        a, b = hgo_copies(k)
        a.wait()
        b.wait_recv()
        b.wait_send()

    @pl.loop(0, Y_UNITS)
    def _(u):
        for m in range(6):
            y_copy(u, m).wait_send()
        yx_copy(u).wait_send()

    @pl.loop(0, X_UNITS)
    def _(v):
        x_copy(v).wait_send()
        for m in range(6):
            xy_copy(v, m).wait_send()

    ag_copy.wait_send()


def shards(local_params, params, momentum, old_mask, attn, resid, gain, out_grad):
    hbm = pl.BlockSpec(memory_space=pl.ANY)
    vmem = pl.BlockSpec(memory_space=pltpu.VMEM)
    smem = pl.BlockSpec(memory_space=pltpu.SMEM)
    dma = pltpu.SemaphoreType.DMA
    gains = gain.astype(F32).reshape(16, 1, 256)
    par, mom, w, hg, at = pl.pallas_call(
        outer_kernel,
        out_shape=(
            jax.ShapeDtypeStruct((128, 512), F32),
            jax.ShapeDtypeStruct((128, 512), F32),
            jax.ShapeDtypeStruct((4, 4, 4, 256, 256), BF),
            jax.ShapeDtypeStruct((8, 1024, 256), BF),
            jax.ShapeDtypeStruct((8, 256, 1024), BF),
        ),
        in_specs=[hbm, hbm, hbm, smem, hbm, hbm, vmem, hbm],
        out_specs=(vmem, vmem, hbm, hbm, hbm),
        scratch_shapes=[
            pltpu.VMEM((8, 128, 512), F32),
            pltpu.VMEM((8, 128, 512), F32),
            pltpu.VMEM((128, 512), F32),
            pltpu.VMEM((8, 128, 512), BF),
            pltpu.VMEM((8, 128, 512), BF),
            pltpu.VMEM((8, 128), F32),
            pltpu.VMEM((16, 8, 128), F32),
            pltpu.VMEM((8, 128), F32),
            pltpu.VMEM((8, 8, 128), F32),
            pltpu.VMEM((2, 128, 256), BF),
            pltpu.VMEM((4, 4, 4, 256, 256), BF),
            pltpu.VMEM((1024, 2048), BF),
            pltpu.VMEM((8, 1024, 256), BF),
            pltpu.VMEM((8, 1024, 256), BF),
            pltpu.VMEM((8, 1024, 256), F32),
            pltpu.VMEM((8, 1024, 256), BF),
            pltpu.VMEM((8, 256, 1024), BF),
            pltpu.VMEM((2, 1024, 128), F32),
            pltpu.VMEM((1024, 128), F32),
            pltpu.VMEM((1024, 128), F32),
            dma((2, 8)), dma, dma((8,)), dma((8,)), dma((16,)), dma((16,)), dma((8,)), dma((8,)), dma, dma,
            dma((17,)), dma((17,)), dma((17,)), dma((36,)), dma((36,)), dma, dma, dma((3,)),
        ],
        compiler_params=pltpu.CompilerParams(
            collective_id=0, has_side_effects=True, vmem_limit_bytes=56 << 20
        ),
        cost_estimate=pl.CostEstimate(flops=9 * 10**9, bytes_accessed=40 * 2**20, transcendentals=0),
        name="outer_step",
    )(local_params[0], params, momentum, old_mask, attn[0], resid[0], gains, out_grad[0])
    wg, ag, hgo = pl.pallas_call(
        grad_kernel,
        out_shape=(
            jax.ShapeDtypeStruct((128, D), BF),
            jax.ShapeDtypeStruct((TOK, HQ), BF),
            jax.ShapeDtypeStruct((TOK, D), BF),
        ),
        in_specs=[hbm, hbm, hbm],
        out_specs=(vmem, vmem, hbm),
        scratch_shapes=[
            pltpu.VMEM((8, 256, 1024), BF),
            pltpu.VMEM((8, 1024, 256), BF),
            pltpu.VMEM((4, 4, 4, 256, 256), BF),
            pltpu.VMEM((8, 2, 4, 2, 128, 256), BF),
            pltpu.VMEM((Y_UNITS, 6, 2, 128, 256), BF),
            pltpu.VMEM((Y_UNITS, 2, 128, 256), BF),
            pltpu.VMEM((X_UNITS, 4, 2, 128, 256), BF),
            pltpu.VMEM((X_UNITS, 6, 128, 256), BF),
            pltpu.VMEM((8, 2, 128, 256), BF),
            pltpu.VMEM((TOK, HQ), F32),
            pltpu.VMEM((TOK, HQ), BF),
            pltpu.VMEM((TOK, HQ), BF),
            dma((3,)), dma((Y_UNITS, 6)), dma((Y_UNITS, 6)), dma((Y_UNITS,)), dma((Y_UNITS,)),
            dma((X_UNITS,)), dma((X_UNITS,)), dma((X_UNITS, 6)), dma((X_UNITS, 6)),
            dma((8,)), dma((8,)), dma, dma, dma((8,)), dma((8,)), dma((8,)),
        ],
        compiler_params=pltpu.CompilerParams(
            collective_id=1, has_side_effects=True, vmem_limit_bytes=56 << 20
        ),
        cost_estimate=pl.CostEstimate(flops=18 * 10**9, bytes_accessed=40 * 2**20, transcendentals=0),
        name="inner_grads",
    )(at, hg, w)
    return (par, mom, wg[None], ag[None], hgo[None])


def solution(mesh):
    return jax.shard_map(
        shards,
        mesh=mesh,
        in_specs=(
            P("replica", "fsdp", None),
            P("fsdp", None),
            P("fsdp", None),
            P(),
            P("replica", "fsdp", None),
            P("replica", "fsdp", None),
            P(),
            P("replica", "fsdp", None),
        ),
        out_specs=(
            P("fsdp", "replica"),
            P("fsdp", "replica"),
            P("replica", "fsdp", None),
            P("replica", "fsdp", None),
            P("replica", "fsdp", None),
        ),
        check_vma=False,
    )
```

time: 458 us -> 173 us (0.38)
  waiting for transfers between devices: 294 us -> 0 us
  Pallas kernels: 0 us -> 162 us
  matrix products: 46.4 us -> 0 us
  local copies, waits for them, and re-layouts: 48.2 us -> 8.91 us
  blocking collectives: 34.9 us -> 0 us
  other arithmetic: 18.2 us -> 1.3 us
  between operations: 15.2 us -> 0.68 us
    pallas_call x0 -> x2, Pallas kernels: none -> 162 us  [the longest x1 97.5 us: shards(): pl.pallas_call(outer_kernel, out_shape=(jax.ShapeDtypeStruct((128, 512),...]
    unnamed x4 -> x0, waiting for transfers between devices: 118 us -> none
    all_gather x1 -> x0, waiting for transfers between devices: 101 us -> none  [shards(): lax.all_gather(full_params.astype(jnp.bfloat16), 'fsdp', axis=0, tiled=True)]
    psum x1 -> x0, waiting for transfers between devices: 74.2 us -> none  [shards(): lax.psum(term.astype(jnp.bfloat16), 'replica').astype(jnp.float32)]
    dot_general x3 -> x0, matrix products: 46.4 us -> none  [the longest x1 17.6 us: shards(): jnp.dot(attn_rows, weights, preferred_element_type=jnp.float32)]
    unnamed x18 -> x11, local copies, waits for them, and re-layouts: 45 us -> 8.91 us
    psum x1 -> x0, blocking collectives: 34.9 us -> none  [shards(): squares = lax.psum(jnp.sum(delta * delta), 'fsdp')]
    convert_element_type x4 -> x0, other arithmetic: 14.2 us -> none  [the longest x1 6.31 us: shards(): full_params.astype(jnp.bfloat16)]
  transfers between devices with their start and end apart: 3 -> 0, of which waited for: 3 -> 0; matrix products, arithmetic and copies ran while one was open for 9% -> 0% of each run, Pallas kernels for 0% -> 0%
where the time goes in v1:
time: 173 us; the launch traced here: 172 us
  Pallas kernels  162 us (94%)
  local copies, waits for them, and re-layouts  8.91 us (5%)
    pallas_call x1, Pallas kernels, shards(): pl.pallas_call(outer_kernel, out_shape=(jax.ShapeDtypeStruct((128, 512),...  97.5 us
    pallas_call x1, Pallas kernels, shards(): pl.pallas_call(grad_kernel, out_shape=(jax.ShapeDtypeStruct((128, D), BF)...  64 us
    unnamed x11, local copies, waits for them, and re-layouts  8.91 us

profile of v1, /device:TPU:1, one launch (start us, length us, event | category | flops | bytes accessed | tf_op | source)
XLA Modules:
  0.0 172.4 jit_solution(13717534651340380586)
XLA Ops:
  0.6 1.3 reshape.17
  1.9 97.5 %outer_step.1 = (f32[128,512]{1,0:T(8,128)}, f32[128,512]{1,0:T(8,128)}, bf16[4,4,4,256,256]{4,3,2,1,0:T(8,128)(2,1)}, bf16[8,1024,256]{2,1,0:T(8,128)(2,1)}, bf16[8,256,1024]{2,1,0:T(8,128)(2,1)}) custom-call(f32[128,4096]{1,0:T(8,128)} %bitcast.14, f32[128,4096]{1,0:T(8,128)} %params.1, f32[128,4096]{1,0:T(8,128)} %momentum.1, s32[8]{0:T(128)} %mask.1, ...), custom_call_target="tpu_custom_call" | custom-call | flops 8999999488 | bytes 41943040 | tf_op jit(solution)/shard_map/outer_step/pallas_call | solution.py:538
  99.4 0.0 copy-start.2
  99.5 0.0 copy-start.1
  99.5 64.0 %inner_grads.1 = (bf16[128,4096]{1,0:T(8,128)(2,1)}, bf16[512,2048]{1,0:T(8,128)(2,1)}, bf16[512,4096]{1,0:T(8,128)(2,1)}) custom-call(bf16[8,256,1024]{2,1,0:T(8,128)(2,1)} %get-tuple-element.15.at, bf16[8,1024,256]{2,1,0:T(8,128)(2,1)} %get-tuple-element.16.hgr, bf16[4,4,4,256,256]{4,3,2,1,0:T(8,128)(2,1)} %get-tuple-element.17.w), custom_call_target="tpu_custom_call" | custom-call | flops 17999998976 | bytes 41943040 | tf_op jit(solution)/shard_map/inner_grads/pallas_call | solution.py:579
  163.5 0.0 copy-start
  163.5 0.0 copy-done.2
  163.5 0.7 copy.18
  164.2 0.0 copy-done.1
  164.2 0.7 copy.19
  164.9 2.3 %copy.20 = bf16[1,128,4096]{2,1,0:T(8,128)(2,1)} copy(bf16[1,128,4096]{2,1,0:T(8,128)(2,1)} %bitcast.10) | data formatting | bytes 2097152
  167.2 3.2 %copy.21 = bf16[1,512,2048]{2,1,0:T(8,128)(2,1)} copy(bf16[1,512,2048]{2,1,0:T(8,128)(2,1)} %bitcast.9) | data formatting | bytes 4194304
  170.4 0.0 copy-done
  170.4 2.0 %copy.22 = bf16[1,512,4096]{2,1,0:T(8,128)(2,1)} copy(bf16[1,512,4096]{2,1,0:T(8,128)(2,1)S(1)} %bitcast.8) | data formatting | bytes 8388608
Async XLA Ops:
  99.4 64.0 %copy-start.2 = (f32[128,512]{1,0:T(8,128)S(1)}, f32[128,512]{1,0:T(8,128)}, u32[]{:S(2)}) copy-start(f32[128,512]{1,0:T(8,128)} %get-tuple-element.26) | copy-start | bytes 786436
  99.5 64.8 %copy-start.1 = (f32[128,512]{1,0:T(8,128)S(1)}, f32[128,512]{1,0:T(8,128)}, u32[]{:S(2)}) copy-start(f32[128,512]{1,0:T(8,128)} %get-tuple-element.27) | copy-start | bytes 786436
  163.5 6.9 %copy-start = (bf16[512,4096]{1,0:T(8,128)(2,1)S(1)}, bf16[512,4096]{1,0:T(8,128)(2,1)}, u32[]{:S(2)}) copy-start(bf16[512,4096]{1,0:T(8,128)(2,1)} %get-tuple-element.20) | copy-start | bytes 12582916

commit v2 on v1

--- a/solution.py
+++ b/solution.py
@@ -22,9 +22,9 @@
 F32 = jnp.float32
 
 PARTS = (
-    (0, 96, 48, ("x", "y", "z")),
-    (96, 80, 48, ("y", "z", "x")),
-    (176, 80, 32, ("z", "x", "y")),
+    (0, 176, 96, ("x", "y", "z")),
+    (176, 160, 80, ("y", "z", "x")),
+    (336, 176, 96, ("z", "x", "y")),
 )
 Y_UNITS = 5
 X_UNITS = 3
@@ -75,23 +75,39 @@
     other = 1 - c
     sibling = device(x, y, z, other)
 
-    order = (4, 1, 2, 3, 5, 6, 7, 0)
+    xl = lax.rem(x, 2)
+
+    def to_replica(k):
+        return (xl + (k // 4) * (1 - 2 * xl)) * 4 + lax.rem(z + k % 4, 4)
+
+    def from_replica(k):
+        return (xl + (k // 4) * (1 - 2 * xl)) * 4 + lax.rem(z + 4 - k % 4, 4)
+
+    order = (6, 2, 5, 7, 1, 3, 4, 0)
     for k in order:
-        cols = pl.ds(pl.multiple_of(lax.rem(r + k, 8) * 512, 512), 512)
+        cols = pl.ds(pl.multiple_of(to_replica(k) * 512, 512), 512)
         pltpu.make_async_copy(lp.at[:, cols], lv.at[k], load_sem.at[0, k]).start()
         pltpu.make_async_copy(params.at[:, cols], pv.at[k], load_sem.at[1, k]).start()
     own_cols = pl.ds(pl.multiple_of(r * 512, 512), 512)
     mom_copy = pltpu.make_async_copy(momentum.at[:, own_cols], mv, mom_sem)
     mom_copy.start()
 
-    targets = [(lax.rem(r + k, 8), f) for k in range(1, 8)]
-    targets += [(r, lax.rem(f + j, 16)) for j in range(1, 16)]
-    outside = jnp.where(lax.rem(x, 2) == 0, down(x), up(x))
-    targets.append(device(outside, y, z, c))
-    greet(targets)
+    def plane_peer(j):
+        return device(lax.rem(x + j // 4, 4), y, lax.rem(z + j % 4, 4), c)
+
+    def column_peer(j):
+        return device(x, lax.rem(y + j // 2, 4), z, c + (j % 2) * (1 - 2 * c))
+
+    greet([plane_peer(j) for j in range(1, 16)] + [column_peer(j) for j in range(1, 8)])
 
     squares = jnp.zeros((8, 512), F32)
     delta_copies = []
+
+    def send_delta(k):
+        copy = remote(dsend.at[k], drecv.at[k], d_send.at[k], d_recv.at[k], (to_replica(k), f))
+        copy.start()
+        delta_copies.append(copy)
+
     for k in order:
         pltpu.make_async_copy(lv.at[k], lv.at[k], load_sem.at[0, k]).wait()
         pltpu.make_async_copy(pv.at[k], pv.at[k], load_sem.at[1, k]).wait()
@@ -102,20 +118,19 @@
             drecv[0] = block
         else:
             dsend[k] = block
-            copy = remote(
-                dsend.at[k], drecv.at[k], d_send.at[k], d_recv.at[k], (lax.rem(r + k, 8), f)
-            )
-            copy.start()
-            delta_copies.append(copy)
+        if k in order[:2]:
+            send_delta(k)
 
     tile = squares[:, 0:128] + squares[:, 128:256] + squares[:, 256:384] + squares[:, 384:512]
     nsend[...] = tile
     nrecv[0] = tile
     norm_copies = []
     for j in range(1, 16):
-        copy = remote(nsend, nrecv.at[j], n_send.at[j], n_recv.at[j], (r, lax.rem(f + j, 16)))
+        copy = remote(nsend, nrecv.at[j], n_send.at[j], n_recv.at[j], plane_peer(j))
         copy.start()
         norm_copies.append(copy)
+    for k in order[2:7]:
+        send_delta(k)
 
     mine = pl.ds(pl.multiple_of(c * TOK, TOK), TOK)
     act_copies = []
@@ -136,133 +151,205 @@
 
     for copy in norm_copies:
         copy.wait_recv()
-    total = jnp.full((8, 128), jnp.sum(nrecv[...]), F32)
-    fsend[...] = total
-    frecv[0] = total
+    partial = jnp.concatenate(
+        [jnp.sum(nrecv[k] + nrecv[k + 8], axis=0, keepdims=True) for k in range(8)], axis=0
+    )
+    fsend[...] = partial
+    frecv[0] = partial
     factor_copies = []
-    for k in range(1, 8):
-        copy = remote(fsend, frecv.at[k], f_send.at[k], f_recv.at[k], (lax.rem(r + k, 8), f))
+    for j in range(1, 8):
+        copy = remote(fsend, frecv.at[j], f_send.at[j], f_recv.at[j], column_peer(j))
         copy.start()
         factor_copies.append(copy)
     for copy in factor_copies:
         copy.wait_recv()
     limit = clip_scale * math.sqrt(HQ * D)
-    factors = jnp.minimum(F32(1.0), limit / (jnp.sqrt(frecv[...]) + 1e-06))
+    norms = jnp.sqrt(jnp.sum(jnp.sum(frecv[...], axis=0), axis=1, keepdims=True))
+    factors = jnp.broadcast_to(jnp.minimum(F32(1.0), limit / (norms + 1e-06)), (8, 128))
     count = F32(0.0)
     for k in range(8):
         count = count + mask[k].astype(F32)
 
+    mom_copy.wait()
     pseudo = jnp.zeros((128, 512), F32)
-    for copy in delta_copies:
-        copy.wait_recv()
-    for k in range(8):
-        weight = mask[lax.rem(r + 8 - k, 8)].astype(F32) * jnp.max(factors[k])
+    for k in (0,) + order[:7]:
+        if k > 0:
+            delta_copies[order.index(k)].wait_recv()
+        weight = mask[from_replica(k)].astype(F32) * jnp.max(factors[k : k + 1])
         pseudo = pseudo + drecv[k].astype(F32) * weight
     pseudo = pseudo / count
-    mom_copy.wait()
     new_mom = outer_beta * mv[...] + pseudo
     new_par = pv[0] - outer_rate * (pseudo + outer_beta * new_mom)
     mom_out[...] = new_mom
     par_out[...] = new_par
     rounded = new_par.astype(BF)
-    wb[0] = rounded[:, 0:256]
-    wb[1] = rounded[:, 256:512]
-
-    rows = pl.ds(pl.multiple_of(c * 128, 128), 128)
-    swap = remote(wb.at[other], w5.at[x, z, y, rows], w_send, w_recv, sibling)
-    swap.start()
-    w5[x, z, y, rows, :] = wb[c]
-    swap.wait_recv()
+    for h in range(2):
+        for q in range(2):
+            wb[h, q] = rounded[:, h * 256 + q * 128 : h * 256 + q * 128 + 128]
+
+    swaps = []
+    for q in range(2):
+        rows = pl.ds(pl.multiple_of(q * 256 + c * 128, 128), 128)
+        swap = remote(wb.at[other, q], w5.at[x, z, y, rows], w_send.at[q], w_recv.at[q], sibling)
+        swap.start()
+        swaps.append(swap)
+        w5[x, z, y, rows, :] = wb[c, q]
+    for swap in swaps:
+        swap.wait_recv()
 
     index = {"x": x, "y": y, "z": z}
-
-    def region(part, gathered, axis, i, half):
-        start, size, cut, _ = PARTS[part]
+    OWN, DOWN, UP, FAR = range(4)
+
+    def at_side(axis, side):
+        i = index[axis]
+        return (i, down(i), up(i), lax.rem(i + 2, 4))[side]
+
+    def region(part, phase, piece, side, half):
+        start, size, cut, axes = PARTS[part]
         if half == 0:
             size = cut
         elif half == 1:
             start, size = start + cut, size - cut
-        at = {a: (slice(None) if a in gathered else index[a]) for a in "xyz"}
-        at[axis] = i
+        at = dict(index)
+        at[axes[phase]] = at_side(axes[phase], side)
+        if phase == 1:
+            at[axes[0]] = at_side(axes[0], piece)
+        if phase == 2:
+            at[axes[0]] = at[axes[1]] = slice(None)
+            if part > 0:
+                at["z"] = at_side("z", piece)
         return w5.at[at["x"], at["z"], at["y"], pl.ds(start, size), :]
 
+    def sem_of(part, phase, piece, kind):
+        return part * 36 + (0, 4, 20)[phase] + piece * 4 + kind
+
     gather_copies = []
 
-    def send(phase, part, kind, ref, axis, i):
-        place_there = dict(index)
-        place_there[axis] = i
-        sem = (phase * 3 + part) * 4 + kind
-        copy = remote(
-            ref, ref, g_send.at[sem], g_recv.at[sem],
-            device(place_there["x"], place_there["y"], place_there["z"], c),
-        )
+    def send(part, phase, piece, kind, ref):
+        axis = PARTS[part][3][phase]
+        to = dict(index)
+        to[axis] = at_side(axis, UP if kind % 2 == 0 else DOWN)
+        sem = sem_of(part, phase, piece, kind)
+        copy = remote(ref, ref, g_send.at[sem], g_recv.at[sem], device(to["x"], to["y"], to["z"], c))
         copy.start()
         gather_copies.append(copy)
 
-    def arrived(phase, part, kind, ref):
-        sem = (phase * 3 + part) * 4 + kind
-        pltpu.make_async_copy(ref, ref, g_recv.at[sem]).wait()
-
-    for phase in range(3):
-        for part in range(3):
-            axes = PARTS[part][3]
-            axis, gathered = axes[phase], axes[:phase]
-            i = index[axis]
-            own = region(part, gathered, axis, i, None)
-            send(phase, part, 0, own, axis, up(i))
-            send(phase, part, 1, own, axis, down(i))
-        if phase == 2:
-            attn_own.wait()
-            attn_send.wait_recv()
-
-            @pl.loop(0, 32)
-            def _(t):
-                tok = pl.ds(pl.multiple_of(lax.rem(t, 4) * 256, 256), 256)
-                col = pl.ds(pl.multiple_of((t // 4) * 256, 256), 256)
-                atv[t // 4, :, tok] = av[tok, col].T
-
-            at_copy = pltpu.make_async_copy(atv, at_out, out_sem.at[0])
-            at_copy.start()
-        for part in range(3):
-            axes = PARTS[part][3]
-            axis, gathered = axes[phase], axes[:phase]
-            i = index[axis]
-            left = region(part, gathered, axis, down(i), None)
-            right = region(part, gathered, axis, up(i), None)
-            arrived(phase, part, 0, left)
-            send(phase, part, 2, region(part, gathered, axis, down(i), 0), axis, up(i))
-            arrived(phase, part, 1, right)
-            send(phase, part, 3, region(part, gathered, axis, up(i), 1), axis, down(i))
-        for part in range(3):
-            axes = PARTS[part][3]
-            axis, gathered = axes[phase], axes[:phase]
-            far = lax.rem(index[axis] + 2, 4)
-            arrived(phase, part, 2, region(part, gathered, axis, far, 0))
-            arrived(phase, part, 3, region(part, gathered, axis, far, 1))
-
-    w_copy = pltpu.make_async_copy(w5, w_out, out_sem.at[1])
-    w_copy.start()
-
+    def arrived(part, phase, piece, kind, ref):
+        pltpu.make_async_copy(ref, ref, g_recv.at[sem_of(part, phase, piece, kind)]).wait()
+
+    def direct(part, phase, piece):
+        ref = region(part, phase, piece, OWN, None)
+        send(part, phase, piece, 0, ref)
+        send(part, phase, piece, 1, ref)
+
+    def sides(part, phase, piece):
+        arrived(part, phase, piece, 0, region(part, phase, piece, DOWN, None))
+        send(part, phase, piece, 2, region(part, phase, piece, DOWN, 0))
+        arrived(part, phase, piece, 1, region(part, phase, piece, UP, None))
+        send(part, phase, piece, 3, region(part, phase, piece, UP, 1))
+
+    def far(part, phase, piece):
+        arrived(part, phase, piece, 2, region(part, phase, piece, FAR, 0))
+        arrived(part, phase, piece, 3, region(part, phase, piece, FAR, 1))
+
+    def hidden(side):
+        plane = at_side("z", side)
+
+        @pl.loop(0, 4)
+        def _(t):
+            half = t // 2
+            k = half * 4 + plane
+            tok = pl.ds(pl.multiple_of(lax.rem(t, 2) * 512, 512), 512)
+
+            def block(xi):
+                both = w5[xi, plane]
+                return jnp.concatenate(
+                    [both[:, 0:256].reshape(1024, 128), both[:, 256:512].reshape(1024, 128)], axis=1
+                )
+
+            h = jnp.dot(av[tok, 0:1024], block(half), preferred_element_type=F32)
+            h = h + jnp.dot(av[tok, 1024:2048], block(half + 2), preferred_element_type=F32)
+            h = h + rv[k, tok, :].astype(F32)
+            hs[k, tok, :] = h
+            sc = ov[k, tok, :].astype(F32) * gain[2 * k + c]
+            hh = h * h
+            sh = sc * h
+            stats[0, tok, :] += hh[:, 0:128] + hh[:, 128:256]
+            stats[1, tok, :] += sh[:, 0:128] + sh[:, 128:256]
+
+    every = range(3)
+    for phase in range(2):
+        for part in every:
+            direct(part, phase, OWN)
+    stats[...] = jnp.zeros_like(stats)
+    for part in every:
+        arrived(part, 0, 0, 0, region(part, 0, 0, DOWN, None))
+        send(part, 0, 0, 2, region(part, 0, 0, DOWN, 0))
+        direct(part, 1, DOWN)
+        arrived(part, 0, 0, 1, region(part, 0, 0, UP, None))
+        send(part, 0, 0, 3, region(part, 0, 0, UP, 1))
+        direct(part, 1, UP)
+    for part in every:
+        far(part, 0, 0)
+        direct(part, 1, FAR)
+    for piece in range(4):
+        for part in every:
+            sides(part, 1, piece)
+    for piece in range(4):
+        for part in every:
+            far(part, 1, piece)
+
+    def turn(start, stop):
+        @pl.loop(start, stop)
+        def _(t):
+            tok = pl.ds(pl.multiple_of(lax.rem(t, 4) * 256, 256), 256)
+            col = pl.ds(pl.multiple_of((t // 4) * 256, 256), 256)
+            atv[t // 4, :, tok] = av[tok, col].T
+
+    direct(1, 2, OWN)
+    direct(2, 2, OWN)
+    direct(0, 2, OWN)
+    direct(1, 2, DOWN)
+    direct(2, 2, DOWN)
+
+    attn_own.wait()
+    attn_send.wait_recv()
+    turn(0, 8)
     for a, b in act_copies:
         a.wait()
         b.wait_recv()
-    stats[...] = jnp.zeros_like(stats)
-
-    @pl.loop(0, 16)
-    def _(t):
-        k = t // 2
-        tok = pl.ds(pl.multiple_of(lax.rem(t, 2) * 512, 512), 512)
-        top = w5[k // 4, lax.rem(k, 4)].reshape(1024, 256)
-        bottom = w5[k // 4 + 2, lax.rem(k, 4)].reshape(1024, 256)
-        h = jnp.dot(av[tok, 0:1024], top, preferred_element_type=F32)
-        h = h + jnp.dot(av[tok, 1024:2048], bottom, preferred_element_type=F32)
-        h = h + rv[k, tok, :].astype(F32)
-        hs[k, tok, :] = h
-        sc = ov[k, tok, :].astype(F32) * gain[2 * k + c]
-        hh = h * h
-        sh = sc * h
-        stats[0, tok, :] += hh[:, 0:128] + hh[:, 128:256]
-        stats[1, tok, :] += sh[:, 0:128] + sh[:, 128:256]
+    sides(1, 2, OWN)
+    sides(2, 2, OWN)
+    direct(1, 2, UP)
+    direct(2, 2, UP)
+    turn(8, 16)
+    sides(1, 2, DOWN)
+    sides(2, 2, DOWN)
+    direct(1, 2, FAR)
+    direct(2, 2, FAR)
+    far(1, 2, OWN)
+    far(2, 2, OWN)
+    hidden(OWN)
+    sides(1, 2, UP)
+    sides(2, 2, UP)
+    sides(0, 2, OWN)
+    far(1, 2, DOWN)
+    far(2, 2, DOWN)
+    hidden(DOWN)
+    sides(1, 2, FAR)
+    sides(2, 2, FAR)
+    far(1, 2, UP)
+    far(2, 2, UP)
+    hidden(UP)
+    turn(16, 32)
+    at_copy = pltpu.make_async_copy(atv, at_out, out_sem.at[0])
+    at_copy.start()
+    far(0, 2, OWN)
+    far(1, 2, FAR)
+    far(2, 2, FAR)
+    w_copy = pltpu.make_async_copy(w5, w_out, out_sem.at[1])
+    w_copy.start()
+    hidden(FAR)
 
     lane = lax.broadcasted_iota(jnp.int32, (256, 128), 1)
 
@@ -290,7 +377,7 @@
     hg_copy = pltpu.make_async_copy(hg, hg_out, out_sem.at[2])
     hg_copy.start()
 
-    for copy in delta_copies + norm_copies + factor_copies + gather_copies + [swap, st_copy, attn_send]:
+    for copy in delta_copies + norm_copies + factor_copies + gather_copies + swaps + [st_copy, attn_send]:
         copy.wait_send()
     for _, b in act_copies:
         b.wait_send()
@@ -441,7 +528,14 @@
     w_load.wait()
 
     def agrad(q, tok):
-        wide = jnp.concatenate([w5[(q // 4) * 2 + k // 4, k % 4, lax.rem(q, 4)] for k in range(8)], axis=1)
+        wide = jnp.concatenate(
+            [
+                w5[(q // 4) * 2 + k // 4, k % 4, lax.rem(q, 4), h * 256 : h * 256 + 256]
+                for k in range(8)
+                for h in range(2)
+            ],
+            axis=1,
+        )
         rows = jnp.concatenate([hgv[k, tok, :] for k in range(8)], axis=1)
         return lax.dot_general(rows, wide, (((1,), (1,)), ((), ())), preferred_element_type=F32)
 
@@ -540,7 +634,7 @@
         out_shape=(
             jax.ShapeDtypeStruct((128, 512), F32),
             jax.ShapeDtypeStruct((128, 512), F32),
-            jax.ShapeDtypeStruct((4, 4, 4, 256, 256), BF),
+            jax.ShapeDtypeStruct((4, 4, 4, 512, 128), BF),
             jax.ShapeDtypeStruct((8, 1024, 256), BF),
             jax.ShapeDtypeStruct((8, 256, 1024), BF),
         ),
@@ -556,8 +650,8 @@
             pltpu.VMEM((16, 8, 128), F32),
             pltpu.VMEM((8, 128), F32),
             pltpu.VMEM((8, 8, 128), F32),
-            pltpu.VMEM((2, 128, 256), BF),
-            pltpu.VMEM((4, 4, 4, 256, 256), BF),
+            pltpu.VMEM((2, 2, 128, 128), BF),
+            pltpu.VMEM((4, 4, 4, 512, 128), BF),
             pltpu.VMEM((1024, 2048), BF),
             pltpu.VMEM((8, 1024, 256), BF),
             pltpu.VMEM((8, 1024, 256), BF),
@@ -567,8 +661,8 @@
             pltpu.VMEM((2, 1024, 128), F32),
             pltpu.VMEM((1024, 128), F32),
             pltpu.VMEM((1024, 128), F32),
-            dma((2, 8)), dma, dma((8,)), dma((8,)), dma((16,)), dma((16,)), dma((8,)), dma((8,)), dma, dma,
-            dma((17,)), dma((17,)), dma((17,)), dma((36,)), dma((36,)), dma, dma, dma((3,)),
+            dma((2, 8)), dma, dma((8,)), dma((8,)), dma((16,)), dma((16,)), dma((8,)), dma((8,)), dma((2,)), dma((2,)),
+            dma((17,)), dma((17,)), dma((17,)), dma((108,)), dma((108,)), dma, dma, dma((3,)),
         ],
         compiler_params=pltpu.CompilerParams(
             collective_id=0, has_side_effects=True, vmem_limit_bytes=56 << 20
@@ -588,7 +682,7 @@
         scratch_shapes=[
             pltpu.VMEM((8, 256, 1024), BF),
             pltpu.VMEM((8, 1024, 256), BF),
-            pltpu.VMEM((4, 4, 4, 256, 256), BF),
+            pltpu.VMEM((4, 4, 4, 512, 128), BF),
             pltpu.VMEM((8, 2, 4, 2, 128, 256), BF),
             pltpu.VMEM((Y_UNITS, 6, 2, 128, 256), BF),
             pltpu.VMEM((Y_UNITS, 2, 128, 256), BF),

time: 173 us -> 156 us (0.902)
  Pallas kernels: 162 us -> 145 us
    pallas_call x1, Pallas kernels: 97.5 us -> 81.7 us  [shards(): pl.pallas_call(outer_kernel, out_shape=(jax.ShapeDtypeStruct((128, 512),...]
where the time goes in v2:
time: 156 us
  Pallas kernels  145 us (93%)
  local copies, waits for them, and re-layouts  8.91 us (6%)
    pallas_call x1, Pallas kernels, shards(): pl.pallas_call(outer_kernel, out_shape=(jax.ShapeDtypeStruct((128, 512),...  81.7 us
    pallas_call x1, Pallas kernels, shards(): pl.pallas_call(grad_kernel, out_shape=(jax.ShapeDtypeStruct((128, D), BF)...  63.5 us
    unnamed x11, local copies, waits for them, and re-layouts  8.91 us

profile of v2, /device:TPU:1, one launch (start us, length us, event | category | flops | bytes accessed | tf_op | source)
XLA Modules:
  0.0 156.1 jit_solution(15782077042168108201)
XLA Ops:
  0.6 1.3 reshape.17
  1.9 81.7 %outer_step.1 = (f32[128,512]{1,0:T(8,128)}, f32[128,512]{1,0:T(8,128)}, bf16[4,4,4,512,128]{4,3,2,1,0:T(8,128)(2,1)}, bf16[8,1024,256]{2,1,0:T(8,128)(2,1)}, bf16[8,256,1024]{2,1,0:T(8,128)(2,1)}) custom-call(f32[128,4096]{1,0:T(8,128)} %bitcast.14, f32[128,4096]{1,0:T(8,128)} %params.1, f32[128,4096]{1,0:T(8,128)} %momentum.1, s32[8]{0:T(128)} %mask.1, ...), custom_call_target="tpu_custom_call" | custom-call | flops 8999999488 | bytes 41943040 | tf_op jit(solution)/shard_map/outer_step/pallas_call | solution.py:632
  83.7 0.0 copy-start.2
  83.7 0.0 copy-start.1
  83.7 63.5 %inner_grads.1 = (bf16[128,4096]{1,0:T(8,128)(2,1)}, bf16[512,2048]{1,0:T(8,128)(2,1)}, bf16[512,4096]{1,0:T(8,128)(2,1)}) custom-call(bf16[8,256,1024]{2,1,0:T(8,128)(2,1)} %get-tuple-element.15.at, bf16[8,1024,256]{2,1,0:T(8,128)(2,1)} %get-tuple-element.16.hgr, bf16[4,4,4,512,128]{4,3,2,1,0:T(8,128)(2,1)} %get-tuple-element.17.w), custom_call_target="tpu_custom_call" | custom-call | flops 17999998976 | bytes 41943040 | tf_op jit(solution)/shard_map/inner_grads/pallas_call | solution.py:673
  147.2 0.0 copy-start
  147.2 0.0 copy-done.2
  147.2 0.7 copy.18
  147.9 0.0 copy-done.1
  147.9 0.7 copy.19
  148.6 2.3 %copy.20 = bf16[1,128,4096]{2,1,0:T(8,128)(2,1)} copy(bf16[1,128,4096]{2,1,0:T(8,128)(2,1)} %bitcast.10) | data formatting | bytes 2097152
  151.0 3.2 %copy.21 = bf16[1,512,2048]{2,1,0:T(8,128)(2,1)} copy(bf16[1,512,2048]{2,1,0:T(8,128)(2,1)} %bitcast.9) | data formatting | bytes 4194304
  154.1 0.0 copy-done
  154.1 2.0 %copy.22 = bf16[1,512,4096]{2,1,0:T(8,128)(2,1)} copy(bf16[1,512,4096]{2,1,0:T(8,128)(2,1)S(1)} %bitcast.8) | data formatting | bytes 8388608
Async XLA Ops:
  83.7 63.5 %copy-start.2 = (f32[128,512]{1,0:T(8,128)S(1)}, f32[128,512]{1,0:T(8,128)}, u32[]{:S(2)}) copy-start(f32[128,512]{1,0:T(8,128)} %get-tuple-element.26) | copy-start | bytes 786436
  83.7 64.2 %copy-start.1 = (f32[128,512]{1,0:T(8,128)S(1)}, f32[128,512]{1,0:T(8,128)}, u32[]{:S(2)}) copy-start(f32[128,512]{1,0:T(8,128)} %get-tuple-element.27) | copy-start | bytes 786436
  147.2 6.9 %copy-start = (bf16[512,4096]{1,0:T(8,128)(2,1)S(1)}, bf16[512,4096]{1,0:T(8,128)(2,1)}, u32[]{:S(2)}) copy-start(bf16[512,4096]{1,0:T(8,128)(2,1)} %get-tuple-element.20) | copy-start | bytes 12582916

commit v3 on v2

--- a/solution.py
+++ b/solution.py
@@ -62,12 +62,15 @@
     pl.semaphore_wait(barrier, len(targets))
 
 
-def outer_kernel(
+def kernel(
     lp, params, momentum, mask, attn, resid, gain, og,
-    par_out, mom_out, w_out, hg_out, at_out,
-    lv, pv, mv, dsend, drecv, nsend, nrecv, fsend, frecv, wb, w5, av, rv, ov, hs, hg, atv, stats, st_own, st_other,
+    par_out, mom_out, wg_out, ag_out, hg_out,
+    lv, pv, mv, dsend, drecv, nsend, nrecv, fsend, frecv, wb, w5, av, rv, ov, hs, atv, stats, st_own, st_other,
+    part, ry, ryx, rx, rxy, ags, agr,
     load_sem, mom_sem, d_send, d_recv, n_send, n_recv, f_send, f_recv, w_send, w_recv,
-    act_own, act_send, act_recv, g_send, g_recv, s_send, s_recv, out_sem,
+    act_own, act_send, act_recv, g_send, g_recv, s_send, s_recv,
+    y_send, y_recv, yx_send, yx_recv, x_send, x_recv, xy_send, xy_recv,
+    fin_own, fin_send, fin_recv, ag_send, ag_recv, ag_own, hgo_own, hgo_send, hgo_recv,
 ):
     x, y, z, c = place()
     r = lax.axis_index("replica")
@@ -115,9 +118,11 @@
         squares = squares + jnp.sum((delta * delta).reshape(16, 8, 512), axis=0)
         block = jnp.clip(delta, -BF16_MAX, BF16_MAX).astype(BF)
         if k == 0:
-            drecv[0] = block
+            drecv[0, 0] = block[:, 0:256]
+            drecv[0, 1] = block[:, 256:512]
         else:
-            dsend[k] = block
+            dsend[k, 0] = block[:, 0:256]
+            dsend[k, 1] = block[:, 256:512]
         if k in order[:2]:
             send_delta(k)
 
@@ -176,7 +181,7 @@
         if k > 0:
             delta_copies[order.index(k)].wait_recv()
         weight = mask[from_replica(k)].astype(F32) * jnp.max(factors[k : k + 1])
-        pseudo = pseudo + drecv[k].astype(F32) * weight
+        pseudo = pseudo + jnp.concatenate([drecv[k, 0], drecv[k, 1]], axis=1).astype(F32) * weight
     pseudo = pseudo / count
     new_mom = outer_beta * mv[...] + pseudo
     new_par = pv[0] - outer_rate * (pseudo + outer_beta * new_mom)
@@ -204,8 +209,8 @@
         i = index[axis]
         return (i, down(i), up(i), lax.rem(i + 2, 4))[side]
 
-    def region(part, phase, piece, side, half):
-        start, size, cut, axes = PARTS[part]
+    def region(p, phase, piece, side, half):
+        start, size, cut, axes = PARTS[p]
         if half == 0:
             size = cut
         elif half == 1:
@@ -216,41 +221,41 @@
             at[axes[0]] = at_side(axes[0], piece)
         if phase == 2:
             at[axes[0]] = at[axes[1]] = slice(None)
-            if part > 0:
+            if p > 0:
                 at["z"] = at_side("z", piece)
         return w5.at[at["x"], at["z"], at["y"], pl.ds(start, size), :]
 
-    def sem_of(part, phase, piece, kind):
-        return part * 36 + (0, 4, 20)[phase] + piece * 4 + kind
+    def sem_of(p, phase, piece, kind):
+        return p * 36 + (0, 4, 20)[phase] + piece * 4 + kind
 
     gather_copies = []
 
-    def send(part, phase, piece, kind, ref):
-        axis = PARTS[part][3][phase]
+    def send(p, phase, piece, kind, ref):
+        axis = PARTS[p][3][phase]
         to = dict(index)
         to[axis] = at_side(axis, UP if kind % 2 == 0 else DOWN)
-        sem = sem_of(part, phase, piece, kind)
+        sem = sem_of(p, phase, piece, kind)
         copy = remote(ref, ref, g_send.at[sem], g_recv.at[sem], device(to["x"], to["y"], to["z"], c))
         copy.start()
         gather_copies.append(copy)
 
-    def arrived(part, phase, piece, kind, ref):
-        pltpu.make_async_copy(ref, ref, g_recv.at[sem_of(part, phase, piece, kind)]).wait()
-
-    def direct(part, phase, piece):
-        ref = region(part, phase, piece, OWN, None)
-        send(part, phase, piece, 0, ref)
-        send(part, phase, piece, 1, ref)
-
-    def sides(part, phase, piece):
-        arrived(part, phase, piece, 0, region(part, phase, piece, DOWN, None))
-        send(part, phase, piece, 2, region(part, phase, piece, DOWN, 0))
-        arrived(part, phase, piece, 1, region(part, phase, piece, UP, None))
-        send(part, phase, piece, 3, region(part, phase, piece, UP, 1))
-
-    def far(part, phase, piece):
-        arrived(part, phase, piece, 2, region(part, phase, piece, FAR, 0))
-        arrived(part, phase, piece, 3, region(part, phase, piece, FAR, 1))
+    def arrived(p, phase, piece, kind, ref):
+        pltpu.make_async_copy(ref, ref, g_recv.at[sem_of(p, phase, piece, kind)]).wait()
+
+    def direct(p, phase, piece):
+        ref = region(p, phase, piece, OWN, None)
+        send(p, phase, piece, 0, ref)
+        send(p, phase, piece, 1, ref)
+
+    def sides(p, phase, piece):
+        arrived(p, phase, piece, 0, region(p, phase, piece, DOWN, None))
+        send(p, phase, piece, 2, region(p, phase, piece, DOWN, 0))
+        arrived(p, phase, piece, 1, region(p, phase, piece, UP, None))
+        send(p, phase, piece, 3, region(p, phase, piece, UP, 1))
+
+    def far(p, phase, piece):
+        arrived(p, phase, piece, 2, region(p, phase, piece, FAR, 0))
+        arrived(p, phase, piece, 3, region(p, phase, piece, FAR, 1))
 
     def hidden(side):
         plane = at_side("z", side)
@@ -271,7 +276,7 @@
             h = h + jnp.dot(av[tok, 1024:2048], block(half + 2), preferred_element_type=F32)
             h = h + rv[k, tok, :].astype(F32)
             hs[k, tok, :] = h
-            sc = ov[k, tok, :].astype(F32) * gain[2 * k + c]
+            sc = ov[k, tok, :].astype(F32) * gain[pl.ds(pl.multiple_of(k * 512 + c * 256, 256), 256)].astype(F32)[None, :]
             hh = h * h
             sh = sc * h
             stats[0, tok, :] += hh[:, 0:128] + hh[:, 128:256]
@@ -279,25 +284,25 @@
 
     every = range(3)
     for phase in range(2):
-        for part in every:
-            direct(part, phase, OWN)
+        for p in every:
+            direct(p, phase, OWN)
     stats[...] = jnp.zeros_like(stats)
-    for part in every:
-        arrived(part, 0, 0, 0, region(part, 0, 0, DOWN, None))
-        send(part, 0, 0, 2, region(part, 0, 0, DOWN, 0))
-        direct(part, 1, DOWN)
-        arrived(part, 0, 0, 1, region(part, 0, 0, UP, None))
-        send(part, 0, 0, 3, region(part, 0, 0, UP, 1))
-        direct(part, 1, UP)
-    for part in every:
-        far(part, 0, 0)
-        direct(part, 1, FAR)
+    for p in every:
+        arrived(p, 0, 0, 0, region(p, 0, 0, DOWN, None))
+        send(p, 0, 0, 2, region(p, 0, 0, DOWN, 0))
+        direct(p, 1, DOWN)
+        arrived(p, 0, 0, 1, region(p, 0, 0, UP, None))
+        send(p, 0, 0, 3, region(p, 0, 0, UP, 1))
+        direct(p, 1, UP)
+    for p in every:
+        far(p, 0, 0)
+        direct(p, 1, FAR)
     for piece in range(4):
-        for part in every:
-            sides(part, 1, piece)
+        for p in every:
+            sides(p, 1, piece)
     for piece in range(4):
-        for part in every:
-            far(part, 1, piece)
+        for p in every:
+            far(p, 1, piece)
 
     def turn(start, stop):
         @pl.loop(start, stop)
@@ -342,13 +347,9 @@
     far(2, 2, UP)
     hidden(UP)
     turn(16, 32)
-    at_copy = pltpu.make_async_copy(atv, at_out, out_sem.at[0])
-    at_copy.start()
     far(0, 2, OWN)
     far(1, 2, FAR)
     far(2, 2, FAR)
-    w_copy = pltpu.make_async_copy(w5, w_out, out_sem.at[1])
-    w_copy.start()
     hidden(FAR)
 
     lane = lax.broadcasted_iota(jnp.int32, (256, 128), 1)
@@ -369,51 +370,28 @@
         tok = pl.ds(pl.multiple_of(t * 256, 256), 256)
         both = (st_own[tok, :] + st_other[tok, :]) * (1.0 / D)
         inv = lax.rsqrt(both[:, 0:1] + 1e-05)
-        slope = inv * inv * inv * both[:, 64:65]
-        for k in range(8):
-            sc = ov[k, tok, :].astype(F32) * gain[2 * k + c]
+        stats[0, tok, :] = jnp.broadcast_to(inv, (256, 128))
+        stats[1, tok, :] = jnp.broadcast_to(inv * inv * inv * both[:, 64:65], (256, 128))
+
+    hg = rv
+
+    def hgrad(k):
+        @pl.loop(0, 4)
+        def _(t):
+            tok = pl.ds(pl.multiple_of(t * 256, 256), 256)
+            sc = ov[k, tok, :].astype(F32) * gain[pl.ds(pl.multiple_of(k * 512 + c * 256, 256), 256)].astype(F32)[None, :]
+            inv = jnp.concatenate([stats[0, tok, :]] * 2, axis=1)
+            slope = jnp.concatenate([stats[1, tok, :]] * 2, axis=1)
             hg[k, tok, :] = (inv * sc - hs[k, tok, :] * slope).astype(BF)
 
-    hg_copy = pltpu.make_async_copy(hg, hg_out, out_sem.at[2])
-    hg_copy.start()
-
-    for copy in delta_copies + norm_copies + factor_copies + gather_copies + swaps + [st_copy, attn_send]:
-        copy.wait_send()
-    for _, b in act_copies:
-        b.wait_send()
-    at_copy.wait()
-    w_copy.wait()
-    hg_copy.wait()
-
-
-def grad_kernel(
-    at, hgr, w,
-    wg_out, ag_out, hg_out,
-    atv, hgv, w5, part, ry, ryx, rx, rxy, fin, agf, ags, agr,
-    load_sem, y_send, y_recv, yx_send, yx_recv, x_send, x_recv, xy_send, xy_recv,
-    fin_send, fin_recv, ag_send, ag_recv, hgo_own, hgo_send, hgo_recv,
-):
-    x, y, z, c = place()
-    other = 1 - c
     xh = x // 2
     xo = 1 - xh
-    sibling = device(x, y, z, other)
     yr, yl, yo = up(y), down(y), lax.rem(y + 2, 4)
     right, left = device(x, yr, z, c), device(x, yl, z, c)
     across = device(lax.rem(x + 2, 4), y, z, c)
 
-    at_load = pltpu.make_async_copy(at, atv, load_sem.at[0])
-    hg_load = pltpu.make_async_copy(hgr, hgv, load_sem.at[1])
-    w_load = pltpu.make_async_copy(w, w5, load_sem.at[2])
-    at_load.start()
-    hg_load.start()
-    w_load.start()
-    greet([sibling, right, left, across])
-    at_load.wait()
-    hg_load.wait()
-
     def comp(k, h, d):
-        acc = jnp.dot(atv[h * 4 + d], hgv[k], preferred_element_type=F32)
+        acc = jnp.dot(atv[h * 4 + d], hg[k], preferred_element_type=F32)
         part[k, h, d] = acc.astype(BF).reshape(2, 128, 256)
 
     def y_copy(u, m):
@@ -435,11 +413,13 @@
         )
 
     def x_start(v):
+        hgrad(Y_UNITS + v)
         for d in range(4):
             comp(Y_UNITS + v, xo, d)
         x_copy(v).start()
 
     def y_start(u):
+        hgrad(u)
         comp(u, 0, yo)
         comp(u, 1, yo)
         y_copy(u, 0).start()
@@ -463,14 +443,13 @@
         comp(u, 1, yl)
         y_copy(u, 3).start()
 
-    mine = pl.ds(pl.multiple_of(c * TOK, TOK), TOK)
     theirs = pl.ds(pl.multiple_of(other * TOK, TOK), TOK)
 
     def hgo_copies(k):
         cols = pl.ds(pl.multiple_of(k * 512 + c * 256, 256), 256)
         return (
-            pltpu.make_async_copy(hgv.at[k, mine], hg_out.at[:, cols], hgo_own.at[k]),
-            remote(hgv.at[k, theirs], hg_out.at[:, cols], hgo_send.at[k], hgo_recv.at[k], sibling),
+            pltpu.make_async_copy(hg.at[k, mine], hg_out.at[:, cols], hgo_own.at[k]),
+            remote(hg.at[k, theirs], hg_out.at[:, cols], hgo_send.at[k], hgo_recv.at[k], sibling),
         )
 
     @pl.loop(0, 8)
@@ -525,8 +504,6 @@
 
     x_middle(0)
 
-    w_load.wait()
-
     def agrad(q, tok):
         wide = jnp.concatenate(
             [
@@ -536,7 +513,7 @@
             ],
             axis=1,
         )
-        rows = jnp.concatenate([hgv[k, tok, :] for k in range(8)], axis=1)
+        rows = jnp.concatenate([hg[k, tok, :] for k in range(8)], axis=1)
         return lax.dot_general(rows, wide, (((1,), (1,)), ((), ())), preferred_element_type=F32)
 
     @pl.loop(0, 8)
@@ -546,16 +523,15 @@
     ag_copy = remote(ags, agr, ag_send, ag_recv, sibling)
     ag_copy.start()
 
-    @pl.loop(0, 8)
-    def _(q):
-        agf[:, pl.ds(pl.multiple_of(q * 256, 256), 256)] = agrad(q, mine)
-
     ag_copy.wait_recv()
 
     @pl.loop(0, 8)
     def _(q):
         col = pl.ds(pl.multiple_of(q * 256, 256), 256)
-        ag_out[:, col] = (agf[:, col] + agr[:, col].astype(F32)).astype(BF)
+        agr[:, col] = (agrad(q, mine) + agr[:, col].astype(F32)).astype(BF)
+
+    ag_store = pltpu.make_async_copy(agr, ag_out, ag_own)
+    ag_store.start()
 
     x_middle(1)
     y_finish(0)
@@ -574,14 +550,21 @@
         add((Y_UNITS + v, xh, yl, 1), rxy[v, 1])
         xy_copy(v, 5).start()
 
-    def fin_copy(k):
+    fin = dsend
+    for copy in delta_copies:
+        copy.wait_send()
+
+    def fin_copies(k):
         cols = pl.ds(pl.multiple_of(k * 512 + c * 256, 256), 256)
-        return remote(fin.at[k, other], wg_out.at[:, cols], fin_send.at[k], fin_recv.at[k], sibling)
+        return (
+            pltpu.make_async_copy(fin.at[k, c], wg_out.at[:, cols], fin_own.at[k]),
+            remote(fin.at[k, other], wg_out.at[:, cols], fin_send.at[k], fin_recv.at[k], sibling),
+        )
 
     def deliver(k):
-        fin_copy(k).start()
-        cols = pl.ds(pl.multiple_of(k * 512 + c * 256, 256), 256)
-        wg_out[:, cols] = fin[k, c]
+        a, b = fin_copies(k)
+        a.start()
+        b.start()
 
     @pl.loop(0, Y_UNITS)
     def _(u):
@@ -600,13 +583,10 @@
 
     @pl.loop(0, 8)
     def _(k):
-        copy = fin_copy(k)
-        copy.wait_recv()
-        copy.wait_send()
-        a, b = hgo_copies(k)
-        a.wait()
-        b.wait_recv()
-        b.wait_send()
+        for a, b in (fin_copies(k), hgo_copies(k)):
+            a.wait()
+            b.wait_recv()
+            b.wait_send()
 
     @pl.loop(0, Y_UNITS)
     def _(u):
@@ -621,6 +601,37 @@
             xy_copy(v, m).wait_send()
 
     ag_copy.wait_send()
+    ag_store.wait()
+    for copy in norm_copies + factor_copies + gather_copies + swaps + [st_copy, attn_send]:
+        copy.wait_send()
+    for _, b in act_copies:
+        b.wait_send()
+
+
+BLOCKS = ((0, 1), (1, 1), (2, 1), (3, 2), (4, 4))
+
+
+def hand_over(*refs):
+    ins, outs, held, in_sem, out_sem = refs[:5], refs[5:10], refs[10:15], refs[15], refs[16]
+    moves = []
+    for i, n in BLOCKS:
+        rows = ins[i].shape[0] // n
+        for j in range(n):
+            at = pl.ds(j * rows, rows)
+            k = len(moves)
+            moves.append(
+                (
+                    pltpu.make_async_copy(ins[i].at[at], held[i].at[at], in_sem.at[k]),
+                    pltpu.make_async_copy(held[i].at[at], outs[i].at[at], out_sem.at[k]),
+                )
+            )
+    for a, _ in moves:
+        a.start()
+    for a, b in moves:
+        a.wait()
+        b.start()
+    for _, b in moves:
+        b.wait()
 
 
 def shards(local_params, params, momentum, old_mask, attn, resid, gain, out_grad):
@@ -628,15 +639,14 @@
     vmem = pl.BlockSpec(memory_space=pltpu.VMEM)
     smem = pl.BlockSpec(memory_space=pltpu.SMEM)
     dma = pltpu.SemaphoreType.DMA
-    gains = gain.astype(F32).reshape(16, 1, 256)
-    par, mom, w, hg, at = pl.pallas_call(
-        outer_kernel,
+    par, mom, wg, ag, hg = pl.pallas_call(
+        kernel,
         out_shape=(
             jax.ShapeDtypeStruct((128, 512), F32),
             jax.ShapeDtypeStruct((128, 512), F32),
-            jax.ShapeDtypeStruct((4, 4, 4, 512, 128), BF),
-            jax.ShapeDtypeStruct((8, 1024, 256), BF),
-            jax.ShapeDtypeStruct((8, 256, 1024), BF),
+            jax.ShapeDtypeStruct((128, D), BF),
+            jax.ShapeDtypeStruct((TOK, HQ), BF),
+            jax.ShapeDtypeStruct((TOK, D), BF),
         ),
         in_specs=[hbm, hbm, hbm, smem, hbm, hbm, vmem, hbm],
         out_specs=(vmem, vmem, hbm, hbm, hbm),
@@ -644,8 +654,8 @@
             pltpu.VMEM((8, 128, 512), F32),
             pltpu.VMEM((8, 128, 512), F32),
             pltpu.VMEM((128, 512), F32),
-            pltpu.VMEM((8, 128, 512), BF),
-            pltpu.VMEM((8, 128, 512), BF),
+            pltpu.VMEM((8, 2, 128, 256), BF),
+            pltpu.VMEM((8, 2, 128, 256), BF),
             pltpu.VMEM((8, 128), F32),
             pltpu.VMEM((16, 8, 128), F32),
             pltpu.VMEM((8, 128), F32),
@@ -656,53 +666,39 @@
             pltpu.VMEM((8, 1024, 256), BF),
             pltpu.VMEM((8, 1024, 256), BF),
             pltpu.VMEM((8, 1024, 256), F32),
-            pltpu.VMEM((8, 1024, 256), BF),
             pltpu.VMEM((8, 256, 1024), BF),
             pltpu.VMEM((2, 1024, 128), F32),
             pltpu.VMEM((1024, 128), F32),
             pltpu.VMEM((1024, 128), F32),
-            dma((2, 8)), dma, dma((8,)), dma((8,)), dma((16,)), dma((16,)), dma((8,)), dma((8,)), dma((2,)), dma((2,)),
-            dma((17,)), dma((17,)), dma((17,)), dma((108,)), dma((108,)), dma, dma, dma((3,)),
-        ],
-        compiler_params=pltpu.CompilerParams(
-            collective_id=0, has_side_effects=True, vmem_limit_bytes=56 << 20
-        ),
-        cost_estimate=pl.CostEstimate(flops=9 * 10**9, bytes_accessed=40 * 2**20, transcendentals=0),
-        name="outer_step",
-    )(local_params[0], params, momentum, old_mask, attn[0], resid[0], gains, out_grad[0])
-    wg, ag, hgo = pl.pallas_call(
-        grad_kernel,
-        out_shape=(
-            jax.ShapeDtypeStruct((128, D), BF),
-            jax.ShapeDtypeStruct((TOK, HQ), BF),
-            jax.ShapeDtypeStruct((TOK, D), BF),
-        ),
-        in_specs=[hbm, hbm, hbm],
-        out_specs=(vmem, vmem, hbm),
-        scratch_shapes=[
-            pltpu.VMEM((8, 256, 1024), BF),
-            pltpu.VMEM((8, 1024, 256), BF),
-            pltpu.VMEM((4, 4, 4, 512, 128), BF),
             pltpu.VMEM((8, 2, 4, 2, 128, 256), BF),
             pltpu.VMEM((Y_UNITS, 6, 2, 128, 256), BF),
             pltpu.VMEM((Y_UNITS, 2, 128, 256), BF),
             pltpu.VMEM((X_UNITS, 4, 2, 128, 256), BF),
             pltpu.VMEM((X_UNITS, 6, 128, 256), BF),
-            pltpu.VMEM((8, 2, 128, 256), BF),
-            pltpu.VMEM((TOK, HQ), F32),
             pltpu.VMEM((TOK, HQ), BF),
             pltpu.VMEM((TOK, HQ), BF),
-            dma((3,)), dma((Y_UNITS, 6)), dma((Y_UNITS, 6)), dma((Y_UNITS,)), dma((Y_UNITS,)),
+            dma((2, 8)), dma, dma((8,)), dma((8,)), dma((16,)), dma((16,)), dma((8,)), dma((8,)), dma((2,)), dma((2,)),
+            dma((17,)), dma((17,)), dma((17,)), dma((108,)), dma((108,)), dma, dma,
+            dma((Y_UNITS, 6)), dma((Y_UNITS, 6)), dma((Y_UNITS,)), dma((Y_UNITS,)),
             dma((X_UNITS,)), dma((X_UNITS,)), dma((X_UNITS, 6)), dma((X_UNITS, 6)),
-            dma((8,)), dma((8,)), dma, dma, dma((8,)), dma((8,)), dma((8,)),
+            dma((8,)), dma((8,)), dma((8,)), dma, dma, dma, dma((8,)), dma((8,)), dma((8,)),
         ],
         compiler_params=pltpu.CompilerParams(
-            collective_id=1, has_side_effects=True, vmem_limit_bytes=56 << 20
+            collective_id=0, has_side_effects=True, vmem_limit_bytes=63 << 20
         ),
-        cost_estimate=pl.CostEstimate(flops=18 * 10**9, bytes_accessed=40 * 2**20, transcendentals=0),
-        name="inner_grads",
-    )(at, hg, w)
-    return (par, mom, wg[None], ag[None], hgo[None])
+        cost_estimate=pl.CostEstimate(flops=26 * 10**9, bytes_accessed=40 * 2**20, transcendentals=0),
+        name="outer_inner",
+    )(local_params[0], params, momentum, old_mask, attn[0], resid[0], gain, out_grad[0])
+    par, mom, wg, ag, hg = pl.pallas_call(
+        hand_over,
+        out_shape=tuple(jax.ShapeDtypeStruct(v.shape, v.dtype) for v in (par, mom, wg, ag, hg)),
+        in_specs=[hbm] * 5,
+        out_specs=(hbm,) * 5,
+        scratch_shapes=[pltpu.VMEM(v.shape, v.dtype) for v in (par, mom, wg, ag, hg)] + [dma((9,)), dma((9,))],
+        compiler_params=pltpu.CompilerParams(vmem_limit_bytes=63 << 20),
+        name="hand_over",
+    )(par, mom, wg, ag, hg)
+    return (par, mom, wg[None], ag[None], hg[None])
 
 
 def solution(mesh):

time: 156 us -> 145 us (0.929)
  local copies, waits for them, and re-layouts: 8.91 us -> 0 us
    unnamed x11 -> x0, local copies, waits for them, and re-layouts: 8.91 us -> none
where the time goes in v3:
time: 145 us; the launch traced here: 144 us
  Pallas kernels  144 us (99%)
    pallas_call x1, Pallas kernels, shards(): pl.pallas_call(kernel, out_shape=(jax.ShapeDtypeStruct((128, 512), F32),...  138 us
    pallas_call x1, Pallas kernels, shards(): pl.pallas_call(hand_over, out_shape=tuple((jax.ShapeDtypeStruct(v.shape,...  6.14 us

profile of v3, /device:TPU:1, one launch (start us, length us, event | category | flops | bytes accessed | tf_op | source)
XLA Modules:
  0.0 144.4 jit_solution(8906044451527923828)
XLA Ops:
  0.6 137.6 %outer_inner.1 = (f32[128,512]{1,0:T(8,128)}, f32[128,512]{1,0:T(8,128)}, bf16[128,4096]{1,0:T(8,128)(2,1)}, bf16[512,2048]{1,0:T(8,128)(2,1)}, bf16[512,4096]{1,0:T(8,128)(2,1)}) custom-call(f32[128,4096]{1,0:T(8,128)} %bitcast.10, f32[128,4096]{1,0:T(8,128)} %params.1, f32[128,4096]{1,0:T(8,128)} %momentum.1, s32[8]{0:T(128)} %mask.1, ...), custom_call_target="tpu_custom_call" | custom-call | flops 25999998976 | bytes 41943040 | tf_op jit(solution)/shard_map/outer_inner/pallas_call | solution.py:642
  138.3 6.1 %hand_over.1 = (f32[128,512]{1,0:T(8,128)}, f32[128,512]{1,0:T(8,128)}, bf16[128,4096]{1,0:T(8,128)(2,1)}, bf16[512,2048]{1,0:T(8,128)(2,1)}, bf16[512,4096]{1,0:T(8,128)(2,1)}) custom-call(f32[128,512]{1,0:T(8,128)} %get-tuple-element.15.refs_0_, f32[128,512]{1,0:T(8,128)} %get-tuple-element.16.refs_1_, bf16[128,4096]{1,0:T(8,128)(2,1)} %get-tuple-element.17.refs_2_, ...), custom_call_target="tpu_custom_call" | custom-call | tf_op jit(solution)/shard_map/hand_over/pallas_call | solution.py:692

commit v4 on v3

v4 whole, which is shorter than its diff:
```python
import functools
import math

import jax
import jax.numpy as jnp
from jax import lax
from jax.experimental import pallas as pl
from jax.experimental.pallas import tpu as pltpu
from jax.sharding import PartitionSpec as P

D = 4096
HQ = 2048
TOK = 512

outer_rate = 0.7
outer_beta = 0.9
clip_scale = 0.1
BF16_MAX = float(jnp.finfo(jnp.bfloat16).max)

MESH = pl.DeviceIdType.MESH
BF = jnp.bfloat16
F32 = jnp.float32

PARTS = (
    (0, 176, 96, ("x", "y", "z")),
    (176, 160, 80, ("y", "z", "x")),
    (336, 176, 96, ("z", "x", "y")),
)
SPLIT = 4

def place():
    r = lax.axis_index("replica")
    f = lax.axis_index("fsdp")
    x = (f // 8) * 2 + r // 4
    return x, lax.rem(f // 2, 4), lax.rem(r, 4), lax.rem(f, 2)


def device(x, y, z, c):
    return (lax.rem(x, 2) * 4 + z, (x // 2) * 8 + y * 2 + c)


def up(i, n=4):
    return lax.rem(i + 1, n)


def down(i, n=4):
    return lax.rem(i + n - 1, n)


def remote(src, dst, send, recv, target):
    return pltpu.make_async_remote_copy(
        src_ref=src, dst_ref=dst, send_sem=send, recv_sem=recv, device_id=target, device_id_type=MESH
    )


def greet(targets):
    barrier = pltpu.get_barrier_semaphore()
    for target in targets:
        pl.semaphore_signal(barrier, inc=1, device_id=target, device_id_type=MESH)
    return lambda: pl.semaphore_wait(barrier, len(targets))


def kernel(
    lp, params, momentum, mask, attn, resid, gain, og,
    par_out, mom_out, wg_out, ag_out, hg_out,
    mv, nsend, nrecv, fsend, frecv, wb, w5, av, rv, ov, hs, atv, stats, st_other,
    part, ry, ryx, rx, rxy,
    load_sem, mom_sem, d_send, d_recv, n_send, n_recv, f_send, f_recv, w_send, w_recv,
    act_own, act_send, act_recv, g_send, g_recv, s_send, s_recv,
    y_send, y_recv, yx_send, yx_recv, x_send, x_recv, xy_send, xy_recv,
    fin_send, fin_recv, ag_send, ag_recv, hgo_own, hgo_send, hgo_recv,
):
    x, y, z, c = place()
    r = lax.axis_index("replica")
    f = lax.axis_index("fsdp")
    other = 1 - c
    sibling = device(x, y, z, other)

    xl = lax.rem(x, 2)

    def to_replica(k):
        return (xl + (k // 4) * (1 - 2 * xl)) * 4 + lax.rem(z + k % 4, 4)

    def from_replica(k):
        return (xl + (k // 4) * (1 - 2 * xl)) * 4 + lax.rem(z + 4 - k % 4, 4)

    order = (6, 2, 5, 7, 1, 3, 4, 0)

    def loads(k):
        out = []
        for h in range(2):
            cols = pl.ds(pl.multiple_of(to_replica(k) * 512 + h * 256, 256), 256)
            for i, src in enumerate((lp, params)):
                dst = hs.at[k, pl.ds(i * 256 + h * 128, 128)]
                out.append(pltpu.make_async_copy(src.at[:, cols], dst, load_sem.at[2 * h + i, k]))
        return out

    for k in order:
        for load in loads(k):
            load.start()
    own_cols = pl.ds(pl.multiple_of(r * 512, 512), 512)
    mom_copy = pltpu.make_async_copy(momentum.at[:, own_cols], mv, mom_sem)
    mom_copy.start()

    def plane_peer(j):
        return device(lax.rem(x + j // 4, 4), y, lax.rem(z + j % 4, 4), c)

    def column_peer(j):
        return device(x, lax.rem(y + j // 2, 4), z, c + (j % 2) * (1 - 2 * c))

    all_here = greet([plane_peer(j) for j in range(1, 16)] + [column_peer(j) for j in range(1, 8)])

    squares = jnp.zeros((8, 256), F32)
    delta_copies = []

    def block_to(k):
        return atv.at[k, pl.ds(128, 128), pl.ds(0, 512)]

    def block_from(k):
        return atv.at[k, pl.ds(0, 128), pl.ds(0, 512)]

    def send_delta(k):
        copy = remote(block_to(k), block_from(k), d_send.at[k], d_recv.at[k], (to_replica(k), f))
        copy.start()
        delta_copies.append(copy)

    for k in order:
        for load in loads(k):
            load.wait()
        for h in range(2):
            delta = hs[k, 256 + h * 128 : 384 + h * 128, :] - hs[k, h * 128 : 128 + h * 128, :]
            squares = squares + jnp.sum((delta * delta).reshape(16, 8, 256), axis=0)
            block = jnp.clip(delta, -BF16_MAX, BF16_MAX).astype(BF)
            row = 0 if k == 0 else 128
            atv[k, row : row + 128, h * 256 : h * 256 + 256] = block

    tile = squares[:, 0:128] + squares[:, 128:256]
    all_here()
    nsend[...] = tile
    nrecv[0] = tile
    norm_copies = []
    for j in range(1, 16):
        copy = remote(nsend, nrecv.at[j], n_send.at[j], n_recv.at[j], plane_peer(j))
        copy.start()
        norm_copies.append(copy)
    for k in order[:7]:
        send_delta(k)

    mine = pl.ds(pl.multiple_of(c * TOK, TOK), TOK)
    act_copies = []
    attn_own = pltpu.make_async_copy(attn, av.at[mine], act_own.at[0])
    attn_send = remote(attn, av.at[mine], act_send.at[0], act_recv.at[0], sibling)
    attn_own.start()
    attn_send.start()
    for k in range(8):
        for s, (src, dst) in enumerate(((resid, rv), (og, ov))):
            here = pl.ds(pl.multiple_of(k * 512 + c * 256, 256), 256)
            there = pl.ds(pl.multiple_of(k * 512 + other * 256, 256), 256)
            i = 1 + 2 * k + s
            a = pltpu.make_async_copy(src.at[:, here], dst.at[k, mine], act_own.at[i])
            b = remote(src.at[:, there], dst.at[k, mine], act_send.at[i], act_recv.at[i], sibling)
            a.start()
            b.start()
            act_copies.append((a, b))

    for copy in norm_copies:
        copy.wait_recv()
    partial = jnp.concatenate(
        [jnp.sum(nrecv[k] + nrecv[k + 8], axis=0, keepdims=True) for k in range(8)], axis=0
    )
    fsend[...] = partial
    frecv[0] = partial
    factor_copies = []
    for j in range(1, 8):
        copy = remote(fsend, frecv.at[j], f_send.at[j], f_recv.at[j], column_peer(j))
        copy.start()
        factor_copies.append(copy)
    for copy in factor_copies:
        copy.wait_recv()
    limit = clip_scale * math.sqrt(HQ * D)
    norms = jnp.sqrt(jnp.sum(jnp.sum(frecv[...], axis=0), axis=1, keepdims=True))
    factors = jnp.broadcast_to(jnp.minimum(F32(1.0), limit / (norms + 1e-06)), (8, 128))
    count = F32(0.0)
    for k in range(8):
        count = count + mask[k].astype(F32)

    mom_copy.wait()
    pseudo = jnp.zeros((128, 512), F32)
    for k in (0,) + order[:7]:
        if k > 0:
            delta_copies[order.index(k)].wait_recv()
        weight = mask[from_replica(k)].astype(F32) * jnp.max(factors[k : k + 1])
        pseudo = pseudo + atv[k, 0:128, 0:512].astype(F32) * weight
    pseudo = pseudo / count
    new_mom = outer_beta * mv[...] + pseudo
    old_par = jnp.concatenate([hs[0, 256:384, :], hs[0, 384:512, :]], axis=1)
    new_par = old_par - outer_rate * (pseudo + outer_beta * new_mom)
    mom_out[...] = new_mom
    par_out[...] = new_par
    rounded = new_par.astype(BF)
    for h in range(2):
        for q in range(2):
            wb[h, q] = rounded[:, h * 256 + q * 128 : h * 256 + q * 128 + 128]

    swaps = []
    for q in range(2):
        rows = pl.ds(pl.multiple_of(q * 256 + c * 128, 128), 128)
        swap = remote(wb.at[other, q], w5.at[x, z, y, rows], w_send.at[q], w_recv.at[q], sibling)
        swap.start()
        swaps.append(swap)
        w5[x, z, y, rows, :] = wb[c, q]
    for swap in swaps:
        swap.wait_recv()

    index = {"x": x, "y": y, "z": z}
    OWN, DOWN, UP, FAR = range(4)

    def at_side(axis, side):
        i = index[axis]
        return (i, down(i), up(i), lax.rem(i + 2, 4))[side]

    def region(p, phase, piece, side, half):
        start, size, cut, axes = PARTS[p]
        if half == 0:
            size = cut
        elif half == 1:
            start, size = start + cut, size - cut
        at = dict(index)
        at[axes[phase]] = at_side(axes[phase], side)
        if phase == 1:
            at[axes[0]] = at_side(axes[0], piece)
        if phase == 2:
            by = "z" if p > 0 else "y"
            at[axes[0]] = at[axes[1]] = slice(None)
            at[by] = at_side(by, piece)
        return w5.at[at["x"], at["z"], at["y"], pl.ds(start, size), :]

    def sem_of(p, phase, piece, kind):
        return p * 36 + (0, 4, 20)[phase] + piece * 4 + kind

    gather_copies = []

    def send(p, phase, piece, kind, ref):
        axis = PARTS[p][3][phase]
        to = dict(index)
        to[axis] = at_side(axis, UP if kind % 2 == 0 else DOWN)
        sem = sem_of(p, phase, piece, kind)
        copy = remote(ref, ref, g_send.at[sem], g_recv.at[sem], device(to["x"], to["y"], to["z"], c))
        copy.start()
        gather_copies.append(copy)

    def arrived(p, phase, piece, kind, ref):
        pltpu.make_async_copy(ref, ref, g_recv.at[sem_of(p, phase, piece, kind)]).wait()

    def direct(p, phase, piece):
        ref = region(p, phase, piece, OWN, None)
        send(p, phase, piece, 0, ref)
        send(p, phase, piece, 1, ref)

    def sides(p, phase, piece):
        arrived(p, phase, piece, 0, region(p, phase, piece, DOWN, None))
        send(p, phase, piece, 2, region(p, phase, piece, DOWN, 0))
        arrived(p, phase, piece, 1, region(p, phase, piece, UP, None))
        send(p, phase, piece, 3, region(p, phase, piece, UP, 1))

    def far(p, phase, piece):
        arrived(p, phase, piece, 2, region(p, phase, piece, FAR, 0))
        arrived(p, phase, piece, 3, region(p, phase, piece, FAR, 1))

    def hidden(side, only=None):
        plane = at_side("z", side)

        @pl.loop(0, 4 if only is None else 2)
        def _(t):
            half = t // 2 if only is None else t
            k = half * 4 + plane
            part_of = lax.rem(t, 2) if only is None else only
            tok = pl.ds(pl.multiple_of(part_of * 512, 512), 512)

            def block(xi):
                both = w5[xi, plane]
                return jnp.concatenate(
                    [both[:, 0:256].reshape(1024, 128), both[:, 256:512].reshape(1024, 128)], axis=1
                )

            h = jnp.dot(av[tok, 0:1024], block(half), preferred_element_type=F32)
            h = h + jnp.dot(av[tok, 1024:2048], block(half + 2), preferred_element_type=F32)
            h = h + rv[k, tok, :].astype(F32)
            hs[k, tok, :] = h
            sc = ov[k, tok, :].astype(F32) * gain[pl.ds(pl.multiple_of(k * 512 + c * 256, 256), 256)].astype(F32)[None, :]
            hh = h * h
            sh = sc * h
            stats[0, tok, :] += hh[:, 0:128] + hh[:, 128:256]
            stats[1, tok, :] += sh[:, 0:128] + sh[:, 128:256]

    every = range(3)
    for phase in range(2):
        for p in every:
            direct(p, phase, OWN)
    stats[...] = jnp.zeros_like(stats)
    for p in every:
        arrived(p, 0, 0, 0, region(p, 0, 0, DOWN, None))
        send(p, 0, 0, 2, region(p, 0, 0, DOWN, 0))
        direct(p, 1, DOWN)
        arrived(p, 0, 0, 1, region(p, 0, 0, UP, None))
        send(p, 0, 0, 3, region(p, 0, 0, UP, 1))
        direct(p, 1, UP)
    for p in every:
        far(p, 0, 0)
        direct(p, 1, FAR)
    for piece in range(4):
        for p in every:
            sides(p, 1, piece)
    for piece in (OWN, DOWN, UP):
        direct(0, 2, piece)
    direct(1, 2, OWN)
    direct(1, 2, DOWN)
    far(2, 1, OWN)
    direct(2, 2, OWN)
    far(2, 1, DOWN)
    direct(2, 2, DOWN)
    for piece in range(4):
        far(0, 1, piece)
    direct(0, 2, FAR)
    for piece in range(4):
        far(1, 1, piece)
    far(2, 1, UP)
    far(2, 1, FAR)

    def turn(start, stop):
        @pl.loop(start, stop)
        def _(t):
            tok = pl.ds(pl.multiple_of(lax.rem(t, 4) * 256, 256), 256)
            col = pl.ds(pl.multiple_of((t // 4) * 256, 256), 256)
            atv[t // 4, :, tok] = av[tok, col].T

    attn_own.wait()
    attn_send.wait_recv()
    for copy in delta_copies:
        copy.wait_send()
    turn(0, 8)
    for a, b in act_copies:
        a.wait()
        b.wait_recv()
    sides(1, 2, OWN)
    sides(2, 2, OWN)
    direct(1, 2, UP)
    direct(2, 2, UP)
    turn(8, 16)
    sides(1, 2, DOWN)
    sides(2, 2, DOWN)
    direct(1, 2, FAR)
    direct(2, 2, FAR)
    far(1, 2, OWN)
    far(2, 2, OWN)
    hidden(OWN)
    sides(1, 2, UP)
    sides(2, 2, UP)
    for piece in range(4):
        sides(0, 2, piece)
    far(1, 2, DOWN)
    far(2, 2, DOWN)
    hidden(DOWN)
    sides(1, 2, FAR)
    sides(2, 2, FAR)
    far(1, 2, UP)
    far(2, 2, UP)
    hidden(UP)
    turn(16, 32)
    for piece in range(4):
        far(0, 2, piece)
    far(1, 2, FAR)
    far(2, 2, FAR)
    lane = lax.broadcasted_iota(jnp.int32, (256, 128), 1)

    def st_copy(t):
        tok = pl.ds(pl.multiple_of(t * 256, 256), 256)
        return remote(stats.at[0, tok], st_other.at[tok], s_send.at[t], s_recv.at[t], sibling)

    def st_start(first):
        @pl.loop(first, first + 2)
        def _(t):
            tok = pl.ds(pl.multiple_of(t * 256, 256), 256)
            a = jnp.sum(stats[0, tok, :], axis=1, keepdims=True)
            b = jnp.sum(stats[1, tok, :], axis=1, keepdims=True)
            stats[0, tok, :] = jnp.where(lane < 64, a, b)
            st_copy(t).start()

    hidden(FAR, 0)
    st_start(0)
    hidden(FAR, 1)
    st_start(2)

    @pl.loop(0, 4)
    def _(t):
        tok = pl.ds(pl.multiple_of(t * 256, 256), 256)
        st_copy(t).wait()
        both = (stats[0, tok, :] + st_other[tok, :]) * (1.0 / D)
        inv = lax.rsqrt(both[:, 0:1] + 1e-05)
        stats[0, tok, :] = jnp.broadcast_to(inv, (256, 128))
        stats[1, tok, :] = jnp.broadcast_to(inv * inv * inv * both[:, 64:65], (256, 128))

    hg = rv

    def hgrad(k):
        @pl.loop(0, 4)
        def _(t):
            tok = pl.ds(pl.multiple_of(t * 256, 256), 256)
            sc = ov[k, tok, :].astype(F32) * gain[pl.ds(pl.multiple_of(k * 512 + c * 256, 256), 256)].astype(F32)[None, :]
            inv = jnp.concatenate([stats[0, tok, :]] * 2, axis=1)
            slope = jnp.concatenate([stats[1, tok, :]] * 2, axis=1)
            hg[k, tok, :] = (inv * sc - hs[k, tok, :] * slope).astype(BF)

    xh = x // 2
    xo = 1 - xh
    yr, yl, yo = up(y), down(y), lax.rem(y + 2, 4)
    right, left = device(x, yr, z, c), device(x, yl, z, c)
    across = device(lax.rem(x + 2, 4), y, z, c)

    def comp(k, h, d):
        acc = jnp.dot(atv[h * 4 + d], hg[k], preferred_element_type=F32).astype(BF)
        part[k, h, d, :, 0] = acc[:, 0:128].reshape(2, 128, 128)
        part[k, h, d, :, 1] = acc[:, 128:256].reshape(2, 128, 128)

    def cut(ref, *index, q):
        return ref.at[index] if q is None else ref.at[(*index, q)]

    def halves(q):
        return (0, 1) if q is None else (q,)

    every_row = slice(None)

    def y_message(m):
        d, h = ((yo, 0), (yo, 1), (yr, 1), (yl, 0), (yr, 0), (yl, 1))[m]
        return d, h, right if m % 2 == 0 else left

    def y_copy(k, m, q=None):
        d, h, target = y_message(m)
        return remote(
            cut(part, k, every_row, d, h, q=q), cut(ry, k, m, every_row, q=q),
            y_send.at[k, m], y_recv.at[k, m], target,
        )

    def yx_copy(k, q=None):
        return remote(
            cut(part, k, xo, y, every_row, q=q), cut(ryx, k, every_row, q=q), yx_send.at[k], yx_recv.at[k], across
        )

    def x_copy(k, q=None):
        v = k - SPLIT
        return remote(
            cut(part, k, xo, every_row, every_row, q=q), cut(rx, v, every_row, every_row, q=q),
            x_send.at[v], x_recv.at[v], across,
        )

    def xy_copy(k, m, q=None):
        v = k - SPLIT
        d, h, target = y_message(m)
        return remote(
            cut(part, k, xh, d, h, q=q), cut(rxy, v, m, q=q), xy_send.at[v, m], xy_recv.at[v, m], target
        )

    def y_start(k):
        hgrad(k)
        comp(k, 0, yo)
        comp(k, 1, yo)
        y_copy(k, 0).start()
        y_copy(k, 1).start()

    y_start(0)

    @pl.loop(1, SPLIT)
    def _(i):
        k = SPLIT + i
        hgrad(k)
        for d in range(4):
            comp(k, xo, d)
        x_copy(k).start()
        y_start(i)

    hgrad(SPLIT)
    for d in (yo, yr, yl, y):
        comp(SPLIT, 0, d)
        comp(SPLIT, 1, d)
        if d is yo:
            y_copy(SPLIT, 0, 0).start()
            y_copy(SPLIT, 1, 0).start()
    x_copy(SPLIT, 1).start()

    @pl.loop(0, SPLIT)
    def _(k):
        comp(k, 0, yr)
        comp(k, 1, yr)
        y_copy(k, 2).start()
        comp(k, 0, yl)
        comp(k, 1, yl)
        y_copy(k, 3).start()

    y_copy(SPLIT, 2, 0).start()
    y_copy(SPLIT, 3, 0).start()

    theirs = pl.ds(pl.multiple_of(other * TOK, TOK), TOK)

    def hgo_copies(k):
        cols = pl.ds(pl.multiple_of(k * 512 + c * 256, 256), 256)
        return (
            pltpu.make_async_copy(hg.at[k, mine], hg_out.at[:, cols], hgo_own.at[k]),
            remote(hg.at[k, theirs], hg_out.at[:, cols], hgo_send.at[k], hgo_recv.at[k], sibling),
        )

    @pl.loop(0, 8)
    def _(k):
        a, b = hgo_copies(k)
        a.start()
        b.start()

    @pl.loop(0, SPLIT)
    def _(k):
        comp(k, 0, y)
        comp(k, 1, y)

    @pl.loop(SPLIT + 1, 8)
    def _(k):
        for d in range(4):
            comp(k, xh, d)

    def add(dst, *srcs):
        total = part[dst].astype(F32)
        for src in srcs:
            total = total + src.astype(F32)
        part[dst] = total.astype(BF)

    def y_middle(k, q=None):
        for m, d, s in ((0, yr, 0), (1, yl, 1)):
            y_copy(k, m, q).wait_recv()
            for h in range(2):
                for j in halves(q):
                    add((k, h, d, s, j), ry[k, m, h, j])
            y_copy(k, m + 4, q).start()

    def y_finish(k, q=None):
        for m in (2, 3, 4, 5):
            y_copy(k, m, q).wait_recv()
        for h in range(2):
            for s, (m, n) in enumerate(((3, 4), (2, 5))):
                for j in halves(q):
                    add((k, h, y, s, j), ry[k, m, h, j], ry[k, n, h, j])
        yx_copy(k, q).start()

    def x_middle(k, q=None):
        v = k - SPLIT
        x_copy(k, q).wait_recv()
        for d in (yo, yr, yl, y):
            for s in range(2):
                for j in halves(q):
                    add((k, xh, d, s, j), rx[v, d, s, j])
            if d is yo:
                xy_copy(k, 0, q).start()
                xy_copy(k, 1, q).start()
        xy_copy(k, 2, q).start()
        xy_copy(k, 3, q).start()

    def xy_middle(k, q=None):
        v = k - SPLIT
        for m, d, s in ((0, yr, 0), (1, yl, 1)):
            xy_copy(k, m, q).wait_recv()
            for j in halves(q):
                add((k, xh, d, s, j), rxy[v, m, j])
            xy_copy(k, m + 4, q).start()

    @pl.loop(0, SPLIT)
    def _(k):
        y_middle(k)

    y_middle(SPLIT, 0)
    x_middle(SPLIT + 1)

    def agrad(q, tok):
        wide = jnp.concatenate(
            [
                w5[(q // 4) * 2 + k // 4, k % 4, lax.rem(q, 4), h * 256 : h * 256 + 256]
                for k in range(8)
                for h in range(2)
            ],
            axis=1,
        )
        rows = jnp.concatenate([hg[k, tok, :] for k in range(8)], axis=1)
        return lax.dot_general(rows, wide, (((1,), (1,)), ((), ())), preferred_element_type=F32)

    ags = av.at[0:TOK]

    @pl.loop(0, 8)
    def _(i):
        ags[:, pl.ds(pl.multiple_of(i * 256, 256), 256)] = agrad(i, theirs).astype(BF)

    ag_copy = remote(ags, ag_out, ag_send, ag_recv, sibling)
    ag_copy.start()
    ag_copy.wait_recv()

    @pl.loop(0, 8)
    def _(i):
        col = pl.ds(pl.multiple_of(i * 256, 256), 256)
        ag_out[:, col] = (agrad(i, mine) + ag_out[:, col].astype(F32)).astype(BF)

    x_middle(SPLIT + 2)
    y_finish(0)
    y_finish(1)
    x_middle(SPLIT + 3)
    xy_middle(SPLIT + 1)
    y_finish(2)
    y_finish(3)
    y_finish(SPLIT, 0)
    xy_middle(SPLIT + 2)
    x_middle(SPLIT, 1)
    xy_middle(SPLIT + 3)
    xy_middle(SPLIT, 1)

    def fin(k, s):
        return av.at[pl.ds(pl.multiple_of(TOK + s * 128, 128), 128), pl.ds(pl.multiple_of(k * 256, 256), 256)]

    def block_columns(k):
        return pl.ds(pl.multiple_of(k * 512 + c * 256, 256), 256)

    def fin_copy(k):
        return remote(
            fin(k, other), wg_out.at[:, block_columns(k)], fin_send.at[k], fin_recv.at[k], sibling
        )

    def y_total(k, j):
        return part[k, xh, y, :, j].astype(F32) + ryx[k, :, j].astype(F32)

    def x_total(k, j):
        v = k - SPLIT
        rows = [
            part[k, xh, y, s, j].astype(F32) + rxy[v, m, j].astype(F32) + rxy[v, n, j].astype(F32)
            for s, (m, n) in enumerate(((3, 4), (2, 5)))
        ]
        return jnp.stack(rows)

    def deliver(k, left_half, right_half):
        total = jnp.concatenate([left_half, right_half], axis=2).astype(BF)
        fin(k, 0)[...] = total[0]
        fin(k, 1)[...] = total[1]
        fin_copy(k).start()
        wg_out[:, block_columns(k)] = fin(k, c)[...]

    def x_arrive(k, q=None):
        for m in (2, 3, 4, 5):
            xy_copy(k, m, q).wait_recv()

    @pl.loop(0, SPLIT)
    def _(k):
        yx_copy(k).wait_recv()
        deliver(k, y_total(k, 0), y_total(k, 1))

    @pl.loop(SPLIT + 1, 8)
    def _(k):
        x_arrive(k)
        deliver(k, x_total(k, 0), x_total(k, 1))

    yx_copy(SPLIT, 0).wait_recv()
    x_arrive(SPLIT, 1)
    deliver(SPLIT, y_total(SPLIT, 0), x_total(SPLIT, 1))

    @pl.loop(0, 8)
    def _(k):
        a, b = hgo_copies(k)
        a.wait()
        for copy in (b, fin_copy(k)):
            copy.wait_recv()
            copy.wait_send()

    def y_drain(k, q=None):
        for m in range(6):
            y_copy(k, m, q).wait_send()
        yx_copy(k, q).wait_send()

    def x_drain(k, q=None):
        x_copy(k, q).wait_send()
        for m in range(6):
            xy_copy(k, m, q).wait_send()

    @pl.loop(0, SPLIT)
    def _(k):
        y_drain(k)

    @pl.loop(SPLIT + 1, 8)
    def _(k):
        x_drain(k)

    y_drain(SPLIT, 0)
    x_drain(SPLIT, 1)

    ag_copy.wait_send()
    for copy in norm_copies + factor_copies + gather_copies + swaps + [attn_send]:
        copy.wait_send()
    for _, b in act_copies:
        b.wait_send()


def hand_over(*refs):
    sems = refs[10]
    copies = [pltpu.make_async_copy(refs[i], refs[5 + i], sems.at[i]) for i in range(5)]
    for copy in copies:
        copy.start()
    for copy in copies:
        copy.wait()


def shards(local_params, params, momentum, old_mask, attn, resid, gain, out_grad):
    hbm = pl.BlockSpec(memory_space=pl.ANY)
    vmem = pl.BlockSpec(memory_space=pltpu.VMEM)
    smem = pl.BlockSpec(memory_space=pltpu.SMEM)
    dma = pltpu.SemaphoreType.DMA
    par, mom, wg, ag, hg = pl.pallas_call(
        kernel,
        out_shape=(
            pltpu.VMEM((128, 512), F32),
            pltpu.VMEM((128, 512), F32),
            pltpu.VMEM((128, D), BF),
            pltpu.VMEM((TOK, HQ), BF),
            pltpu.VMEM((TOK, D), BF),
        ),
        in_specs=[hbm, hbm, hbm, smem, hbm, hbm, vmem, hbm],
        out_specs=(vmem,) * 5,
        scratch_shapes=[
            pltpu.VMEM((128, 512), F32),
            pltpu.VMEM((8, 128), F32),
            pltpu.VMEM((16, 8, 128), F32),
            pltpu.VMEM((8, 128), F32),
            pltpu.VMEM((8, 8, 128), F32),
            pltpu.VMEM((2, 2, 128, 128), BF),
            pltpu.VMEM((4, 4, 4, 512, 128), BF),
            pltpu.VMEM((1024, 2048), BF),
            pltpu.VMEM((8, 1024, 256), BF),
            pltpu.VMEM((8, 1024, 256), BF),
            pltpu.VMEM((8, 1024, 256), F32),
            pltpu.VMEM((8, 256, 1024), BF),
            pltpu.VMEM((2, 1024, 128), F32),
            pltpu.VMEM((1024, 128), F32),
            pltpu.VMEM((8, 2, 4, 2, 2, 128, 128), BF),
            pltpu.VMEM((SPLIT + 1, 6, 2, 2, 128, 128), BF),
            pltpu.VMEM((SPLIT + 1, 2, 2, 128, 128), BF),
            pltpu.VMEM((8 - SPLIT, 4, 2, 2, 128, 128), BF),
            pltpu.VMEM((8 - SPLIT, 6, 2, 128, 128), BF),
            dma((4, 8)), dma, dma((8,)), dma((8,)), dma((16,)), dma((16,)), dma((8,)), dma((8,)), dma((2,)), dma((2,)),
            dma((17,)), dma((17,)), dma((17,)), dma((108,)), dma((108,)), dma((4,)), dma((4,)),
            dma((SPLIT + 1, 6)), dma((SPLIT + 1, 6)), dma((SPLIT + 1,)), dma((SPLIT + 1,)),
            dma((8 - SPLIT,)), dma((8 - SPLIT,)), dma((8 - SPLIT, 6)), dma((8 - SPLIT, 6)),
            dma((8,)), dma((8,)), dma, dma, dma((8,)), dma((8,)), dma((8,)),
        ],
        compiler_params=pltpu.CompilerParams(
            collective_id=0, has_side_effects=True, vmem_limit_bytes=54 << 20
        ),
        cost_estimate=pl.CostEstimate(flops=26 * 10**9, bytes_accessed=40 * 2**20, transcendentals=0),
        name="outer_inner",
    )(local_params[0], params, momentum, old_mask, attn[0], resid[0], gain, out_grad[0])
    par, mom, wg, ag, hg = pl.pallas_call(
        hand_over,
        out_shape=tuple(jax.ShapeDtypeStruct(v.shape, v.dtype) for v in (par, mom, wg, ag, hg)),
        in_specs=[vmem] * 5,
        out_specs=(hbm,) * 5,
        scratch_shapes=[dma((5,))],
        compiler_params=pltpu.CompilerParams(vmem_limit_bytes=1 << 20),
        name="hand_over",
    )(*(pltpu.with_memory_space_constraint(v, pltpu.VMEM) for v in (par, mom, wg, ag, hg)))
    return (par, mom, wg[None], ag[None], hg[None])


def solution(mesh):
    return jax.shard_map(
        shards,
        mesh=mesh,
        in_specs=(
            P("replica", "fsdp", None),
            P("fsdp", None),
            P("fsdp", None),
            P(),
            P("replica", "fsdp", None),
            P("replica", "fsdp", None),
            P(),
            P("replica", "fsdp", None),
        ),
        out_specs=(
            P("fsdp", "replica"),
            P("fsdp", "replica"),
            P("replica", "fsdp", None),
            P("replica", "fsdp", None),
            P("replica", "fsdp", None),
        ),
        check_vma=False,
    )
```

time: 145 us -> 138 us (0.952)
  Pallas kernels: 144 us -> 137 us
    pallas_call x1, Pallas kernels: 138 us -> 133 us  [shards(): pl.pallas_call(kernel, out_shape=(pltpu.VMEM((128, 512), F32), pltpu.VMEM...]
    pallas_call x1, Pallas kernels: 6.14 us -> 3.27 us  [shards(): pl.pallas_call(hand_over, out_shape=tuple((jax.ShapeDtypeStruct(v.shape,...]
where the time goes in v4:
time: 138 us; the launch traced here: 137 us
  Pallas kernels  137 us (99%)
    pallas_call x1, Pallas kernels, shards(): pl.pallas_call(kernel, out_shape=(pltpu.VMEM((128, 512), F32), pltpu.VMEM...  133 us
    pallas_call x1, Pallas kernels, shards(): pl.pallas_call(hand_over, out_shape=tuple((jax.ShapeDtypeStruct(v.shape,...  3.27 us

profile of v4, /device:TPU:1, one launch (start us, length us, event | category | flops | bytes accessed | tf_op | source)
XLA Modules:
  0.0 137.4 jit_solution(10141269945444348818)
XLA Ops:
  0.6 133.5 %outer_inner.1 = (f32[128,512]{1,0:T(8,128)S(1)}, f32[128,512]{1,0:T(8,128)S(1)}, bf16[128,4096]{1,0:T(8,128)(2,1)S(1)}, bf16[512,2048]{1,0:T(8,128)(2,1)S(1)}, bf16[512,4096]{1,0:T(8,128)(2,1)S(1)}) custom-call(f32[128,4096]{1,0:T(8,128)} %bitcast.10, f32[128,4096]{1,0:T(8,128)} %params.1, f32[128,4096]{1,0:T(8,128)} %momentum.1, s32[8]{0:T(128)} %mask.1, ...), custom_call_target="tpu_custom_call" | custom-call | flops 25999998976 | bytes 41943040 | tf_op jit(solution)/shard_map/outer_inner/pallas_call | solution.py:715
  134.1 3.3 %hand_over.1 = (f32[128,512]{1,0:T(8,128)}, f32[128,512]{1,0:T(8,128)}, bf16[128,4096]{1,0:T(8,128)(2,1)}, bf16[512,2048]{1,0:T(8,128)(2,1)}, bf16[512,4096]{1,0:T(8,128)(2,1)}) custom-call(f32[128,512]{1,0:T(8,128)S(1)} %get-tuple-element.15.refs_0_, f32[128,512]{1,0:T(8,128)S(1)} %get-tuple-element.16.refs_1_, ...), custom_call_target="tpu_custom_call" | custom-call | tf_op jit(solution)/shard_map/hand_over/pallas_call | solution.py:758

commit v5 on v4

--- a/solution.py
+++ b/solution.py
@@ -63,9 +63,9 @@
 def kernel(
     lp, params, momentum, mask, attn, resid, gain, og,
     par_out, mom_out, wg_out, ag_out, hg_out,
-    mv, nsend, nrecv, fsend, frecv, wb, w5, av, rv, ov, hs, atv, stats, st_other,
+    mv, pv, nsend, nrecv, fsend, frecv, w5, av, rv, ov, hs, atv, stats, st_other,
     part, ry, ryx, rx, rxy,
-    load_sem, mom_sem, d_send, d_recv, n_send, n_recv, f_send, f_recv, w_send, w_recv,
+    load_sem, old_sem, old_send, old_recv, new_send, new_recv, d_send, d_recv, n_send, n_recv, f_send, f_recv,
     act_own, act_send, act_recv, g_send, g_recv, s_send, s_recv,
     y_send, y_recv, yx_send, yx_recv, x_send, x_recv, xy_send, xy_recv,
     fin_send, fin_recv, ag_send, ag_recv, hgo_own, hgo_send, hgo_recv,
@@ -98,9 +98,21 @@
     for k in order:
         for load in loads(k):
             load.start()
-    own_cols = pl.ds(pl.multiple_of(r * 512, 512), 512)
-    mom_copy = pltpu.make_async_copy(momentum.at[:, own_cols], mv, mom_sem)
-    mom_copy.start()
+
+    def half_columns(h):
+        return pl.ds(pl.multiple_of(r * 512 + h * 256, 256), 256)
+
+    def old_copies(src, dst, i):
+        return (
+            pltpu.make_async_copy(src.at[:, half_columns(c)], dst.at[:, pl.ds(0, 256)], old_sem.at[i]),
+            remote(
+                src.at[:, half_columns(other)], dst.at[:, pl.ds(256, 256)], old_send.at[i], old_recv.at[i], sibling
+            ),
+        )
+
+    old_pairs = [old_copies(momentum, mv, 0), old_copies(params, pv, 1)]
+    for own_old, _ in old_pairs:
+        own_old.start()
 
     def plane_peer(j):
         return device(lax.rem(x + j // 4, 4), y, lax.rem(z + j % 4, 4), c)
@@ -108,19 +120,23 @@
     def column_peer(j):
         return device(x, lax.rem(y + j // 2, 4), z, c + (j % 2) * (1 - 2 * c))
 
-    all_here = greet([plane_peer(j) for j in range(1, 16)] + [column_peer(j) for j in range(1, 8)])
+    def block_peer(k, dc):
+        return (to_replica(k), f + dc * (1 - 2 * c))
+
+    all_here = greet(
+        [plane_peer(j) for j in range(1, 16)]
+        + [column_peer(j) for j in range(1, 8)]
+        + [block_peer(k, 1) for k in range(1, 8)]
+    )
 
     squares = jnp.zeros((8, 256), F32)
     delta_copies = []
 
-    def block_to(k):
-        return atv.at[k, pl.ds(128, 128), pl.ds(0, 512)]
-
-    def block_from(k):
-        return atv.at[k, pl.ds(0, 128), pl.ds(0, 512)]
-
-    def send_delta(k):
-        copy = remote(block_to(k), block_from(k), d_send.at[k], d_recv.at[k], (to_replica(k), f))
+    def send_delta(k, dc):
+        half = c + dc * (1 - 2 * c)
+        src = atv.at[k, pl.ds(128, 128), pl.ds(pl.multiple_of(half * 256, 256), 256)]
+        dst = atv.at[k, pl.ds(0, 128), pl.ds(dc * 256, 256)]
+        copy = remote(src, dst, d_send.at[2 * k + dc], d_recv.at[2 * k + dc], block_peer(k, dc))
         copy.start()
         delta_copies.append(copy)
 
@@ -131,8 +147,8 @@
             delta = hs[k, 256 + h * 128 : 384 + h * 128, :] - hs[k, h * 128 : 128 + h * 128, :]
             squares = squares + jnp.sum((delta * delta).reshape(16, 8, 256), axis=0)
             block = jnp.clip(delta, -BF16_MAX, BF16_MAX).astype(BF)
-            row = 0 if k == 0 else 128
-            atv[k, row : row + 128, h * 256 : h * 256 + 256] = block
+            atv[k, 128:256, h * 256 : h * 256 + 256] = block
+    atv[0, 0:128, 0:256] = atv[0, 128:256, pl.ds(pl.multiple_of(c * 256, 256), 256)]
 
     tile = squares[:, 0:128] + squares[:, 128:256]
     all_here()
@@ -144,7 +160,11 @@
         copy.start()
         norm_copies.append(copy)
     for k in order[:7]:
-        send_delta(k)
+        for dc in range(2):
+            send_delta(k, dc)
+    send_delta(0, 1)
+    for _, sent_old in old_pairs:
+        sent_old.start()
 
     mine = pl.ds(pl.multiple_of(c * TOK, TOK), TOK)
     act_copies = []
@@ -184,33 +204,24 @@
     for k in range(8):
         count = count + mask[k].astype(F32)
 
-    mom_copy.wait()
     pseudo = jnp.zeros((128, 512), F32)
-    for k in (0,) + order[:7]:
-        if k > 0:
-            delta_copies[order.index(k)].wait_recv()
+    for copy in delta_copies:
+        copy.wait_recv()
+    for k in range(8):
         weight = mask[from_replica(k)].astype(F32) * jnp.max(factors[k : k + 1])
         pseudo = pseudo + atv[k, 0:128, 0:512].astype(F32) * weight
     pseudo = pseudo / count
+    for own_old, sent_old in old_pairs:
+        own_old.wait()
+        sent_old.wait_recv()
     new_mom = outer_beta * mv[...] + pseudo
-    old_par = jnp.concatenate([hs[0, 256:384, :], hs[0, 384:512, :]], axis=1)
-    new_par = old_par - outer_rate * (pseudo + outer_beta * new_mom)
-    mom_out[...] = new_mom
-    par_out[...] = new_par
+    new_par = pv[...] - outer_rate * (pseudo + outer_beta * new_mom)
     rounded = new_par.astype(BF)
-    for h in range(2):
+
+    for dc in range(2):
         for q in range(2):
-            wb[h, q] = rounded[:, h * 256 + q * 128 : h * 256 + q * 128 + 128]
-
-    swaps = []
-    for q in range(2):
-        rows = pl.ds(pl.multiple_of(q * 256 + c * 128, 128), 128)
-        swap = remote(wb.at[other, q], w5.at[x, z, y, rows], w_send.at[q], w_recv.at[q], sibling)
-        swap.start()
-        swaps.append(swap)
-        w5[x, z, y, rows, :] = wb[c, q]
-    for swap in swaps:
-        swap.wait_recv()
+            rows = pl.ds(pl.multiple_of(q * 256 + (c + dc * (1 - 2 * c)) * 128, 128), 128)
+            w5[x, z, y, rows, :] = rounded[:, dc * 256 + q * 128 : dc * 256 + q * 128 + 128]
 
     index = {"x": x, "y": y, "z": z}
     OWN, DOWN, UP, FAR = range(4)
@@ -298,6 +309,17 @@
         for p in every:
             direct(p, phase, OWN)
     stats[...] = jnp.zeros_like(stats)
+
+    here = pl.ds(pl.multiple_of(c * 256, 256), 256)
+    mom_out[:, here] = new_mom[:, 0:256]
+    par_out[:, here] = new_par[:, 0:256]
+    mv[:, 256:512] = new_mom[:, 256:512]
+    pv[:, 256:512] = new_par[:, 256:512]
+    new_copies = []
+    for i, (src, dst) in enumerate(((mv, mom_out), (pv, par_out))):
+        copy = remote(src.at[:, pl.ds(256, 256)], dst.at[:, here], new_send.at[i], new_recv.at[i], sibling)
+        copy.start()
+        new_copies.append(copy)
     for p in every:
         arrived(p, 0, 0, 0, region(p, 0, 0, DOWN, None))
         send(p, 0, 0, 2, region(p, 0, 0, DOWN, 0))
@@ -692,8 +714,12 @@
     x_drain(SPLIT, 1)
 
     ag_copy.wait_send()
-    for copy in norm_copies + factor_copies + gather_copies + swaps + [attn_send]:
+    for copy in norm_copies + factor_copies + gather_copies + [attn_send]:
         copy.wait_send()
+    for _, sent_old in old_pairs:
+        sent_old.wait_send()
+    for copy in new_copies:
+        copy.wait()
     for _, b in act_copies:
         b.wait_send()
 
@@ -725,11 +751,11 @@
         out_specs=(vmem,) * 5,
         scratch_shapes=[
             pltpu.VMEM((128, 512), F32),
+            pltpu.VMEM((128, 512), F32),
             pltpu.VMEM((8, 128), F32),
             pltpu.VMEM((16, 8, 128), F32),
             pltpu.VMEM((8, 128), F32),
             pltpu.VMEM((8, 8, 128), F32),
-            pltpu.VMEM((2, 2, 128, 128), BF),
             pltpu.VMEM((4, 4, 4, 512, 128), BF),
             pltpu.VMEM((1024, 2048), BF),
             pltpu.VMEM((8, 1024, 256), BF),
@@ -743,7 +769,8 @@
             pltpu.VMEM((SPLIT + 1, 2, 2, 128, 128), BF),
             pltpu.VMEM((8 - SPLIT, 4, 2, 2, 128, 128), BF),
             pltpu.VMEM((8 - SPLIT, 6, 2, 128, 128), BF),
-            dma((4, 8)), dma, dma((8,)), dma((8,)), dma((16,)), dma((16,)), dma((8,)), dma((8,)), dma((2,)), dma((2,)),
+            dma((4, 8)), dma((2,)), dma((2,)), dma((2,)), dma((2,)), dma((2,)),
+            dma((16,)), dma((16,)), dma((16,)), dma((16,)), dma((8,)), dma((8,)),
             dma((17,)), dma((17,)), dma((17,)), dma((108,)), dma((108,)), dma((4,)), dma((4,)),
             dma((SPLIT + 1, 6)), dma((SPLIT + 1, 6)), dma((SPLIT + 1,)), dma((SPLIT + 1,)),
             dma((8 - SPLIT,)), dma((8 - SPLIT,)), dma((8 - SPLIT, 6)), dma((8 - SPLIT, 6)),

time: 138 us -> 136 us (0.986)
  no operation moved by 1% of the time
where the time goes in v5:
time: 136 us
  Pallas kernels  136 us (100%)
    pallas_call x1, Pallas kernels, shards(): pl.pallas_call(kernel, out_shape=(pltpu.VMEM((128, 512), F32), pltpu.VMEM...  132 us
    pallas_call x1, Pallas kernels, shards(): pl.pallas_call(hand_over, out_shape=tuple((jax.ShapeDtypeStruct(v.shape,...  3.27 us

profile of v5, /device:TPU:1, one launch (start us, length us, event | category | flops | bytes accessed | tf_op | source)
XLA Modules:
  0.0 136.3 jit_solution(2689072362082602252)
XLA Ops:
  0.6 132.3 %outer_inner.1 = (f32[128,512]{1,0:T(8,128)S(1)}, f32[128,512]{1,0:T(8,128)S(1)}, bf16[128,4096]{1,0:T(8,128)(2,1)S(1)}, bf16[512,2048]{1,0:T(8,128)(2,1)S(1)}, bf16[512,4096]{1,0:T(8,128)(2,1)S(1)}) custom-call(f32[128,4096]{1,0:T(8,128)} %bitcast.10, f32[128,4096]{1,0:T(8,128)} %params.1, f32[128,4096]{1,0:T(8,128)} %momentum.1, s32[8]{0:T(128)} %mask.1, ...), custom_call_target="tpu_custom_call" | custom-call | flops 25999998976 | bytes 41943040 | tf_op jit(solution)/shard_map/outer_inner/pallas_call | solution.py:741
  132.9 3.3 %hand_over.1 = (f32[128,512]{1,0:T(8,128)}, f32[128,512]{1,0:T(8,128)}, bf16[128,4096]{1,0:T(8,128)(2,1)}, bf16[512,2048]{1,0:T(8,128)(2,1)}, bf16[512,4096]{1,0:T(8,128)(2,1)}) custom-call(f32[128,512]{1,0:T(8,128)S(1)} %get-tuple-element.15.refs_0_, f32[128,512]{1,0:T(8,128)S(1)} %get-tuple-element.16.refs_1_, ...), custom_call_target="tpu_custom_call" | custom-call | tf_op jit(solution)/shard_map/hand_over/pallas_call | solution.py:785

commit v6 on v5

--- a/solution.py
+++ b/solution.py
@@ -376,6 +376,7 @@
     far(1, 2, OWN)
     far(2, 2, OWN)
     hidden(OWN)
+    turn(16, 24)
     sides(1, 2, UP)
     sides(2, 2, UP)
     for piece in range(4):
@@ -383,12 +384,12 @@
     far(1, 2, DOWN)
     far(2, 2, DOWN)
     hidden(DOWN)
+    turn(24, 32)
     sides(1, 2, FAR)
     sides(2, 2, FAR)
     far(1, 2, UP)
     far(2, 2, UP)
     hidden(UP)
-    turn(16, 32)
     for piece in range(4):
         far(0, 2, piece)
     far(1, 2, FAR)

time: 136 us -> 135 us (level)
  Pallas kernels: 136 us -> 134 us
where the time goes in v6:
time: 135 us
  Pallas kernels  134 us (99%)
    pallas_call x1, Pallas kernels, shards(): pl.pallas_call(kernel, out_shape=(pltpu.VMEM((128, 512), F32), pltpu.VMEM...  131 us
    pallas_call x1, Pallas kernels, shards(): pl.pallas_call(hand_over, out_shape=tuple((jax.ShapeDtypeStruct(v.shape,...  3.27 us

profile of v6, /device:TPU:1, one launch (start us, length us, event | category | flops | bytes accessed | tf_op | source)
XLA Modules:
  0.0 135.2 jit_solution(9544530554464321608)
XLA Ops:
  0.6 131.1 %outer_inner.1 = (f32[128,512]{1,0:T(8,128)S(1)}, f32[128,512]{1,0:T(8,128)S(1)}, bf16[128,4096]{1,0:T(8,128)(2,1)S(1)}, bf16[512,2048]{1,0:T(8,128)(2,1)S(1)}, bf16[512,4096]{1,0:T(8,128)(2,1)S(1)}) custom-call(f32[128,4096]{1,0:T(8,128)} %bitcast.10, f32[128,4096]{1,0:T(8,128)} %params.1, f32[128,4096]{1,0:T(8,128)} %momentum.1, s32[8]{0:T(128)} %mask.1, ...), custom_call_target="tpu_custom_call" | custom-call | flops 25999998976 | bytes 41943040 | tf_op jit(solution)/shard_map/outer_inner/pallas_call | solution.py:742
  131.7 3.3 %hand_over.1 = (f32[128,512]{1,0:T(8,128)}, f32[128,512]{1,0:T(8,128)}, bf16[128,4096]{1,0:T(8,128)(2,1)}, bf16[512,2048]{1,0:T(8,128)(2,1)}, bf16[512,4096]{1,0:T(8,128)(2,1)}) custom-call(f32[128,512]{1,0:T(8,128)S(1)} %get-tuple-element.15.refs_0_, f32[128,512]{1,0:T(8,128)S(1)} %get-tuple-element.16.refs_1_, ...), custom_call_target="tpu_custom_call" | custom-call | tf_op jit(solution)/shard_map/hand_over/pallas_call | solution.py:786
